TPU v7x, 256 devices: a whole 4x4x8 slice. The times are simulated.
256 devices in a mesh: db: 32 (over x, z), mp: 4 (over y), section: 2 (over core).
Axes of the slice: x: 4, y: 4, z: 8, core: 2. Of those that a mesh axis runs over, the one named last changes fastest.
Arguments:
- queries: bfloat16 [16384, 8192], P('db', ('mp', 'section')), may hold values from -6 to 6
- database: bfloat16 [128, 1024, 1024], P(None, 'db', ('mp', 'section')), may hold values from -6 to 6
- neighbour_ids: int32 [256, 2], P('db'), may hold values from 0 to 1023, as said below
- live_counts: int32 [256], P('db'), may hold values from 1 to 2
- entry_rows: int32 [1024], replicated, may hold values from 0 to 1023, as said below
- enc_gain: float32 [2, 1024], replicated, may hold values from 0.1 to 1.9
- enc_qkv: bfloat16 [2, 1024, 3, 1024], P(None, None, None, ('mp', 'section')), may hold values from -0.1875 to 0.1875
- enc_out: bfloat16 [2, 1024, 1024], replicated, may hold values from -0.1875 to 0.1875
- final_gain: float32 [1024], replicated, may hold values from 0.1 to 1.9
- kv_weight: bfloat16 [1024, 2, 8192], P(None, None, ('mp', 'section')), may hold values from -0.1875 to 0.1875
Outputs:
- retrieved: bfloat16 [16384, 8192], P('db', ('mp', 'section'))
Inputs may be any that keep to these rules, and one draw needn't show every extreme that they name: `neighbour_ids`: entry c lies on db shard entry_rows[c] // 32. Of the 16 ids in the rows of one db index, at most 2 lie on one shard; one shard, the same for all db indices, holds exactly 2 of every db index's ids, and at least one other shard holds exactly 2 too. `entry_rows`: A permutation of the entry ids.
All inputs are finite; a program needn't handle non-finite values.
Results may differ from a plain program's by a relative error of at most 0.035.
Values may be sent and summed in bfloat16 or wider, within the bound.
A program may use at most 128 MiB of HBM per device.

v0:
```python
import math

import jax
import jax.numpy as jnp
from jax import lax
from jax.sharding import PartitionSpec as P

BL = 64


def unit_heads(tensor):
    return tensor * lax.rsqrt(jnp.mean(tensor * tensor, axis=-1, keepdims=True) + 1e-06)


def gather_rows(tensor, project):
    return project(lax.all_gather(tensor, ("mp", "section"), axis=0, tiled=True), jnp.int32(0))


def on_device(
    queries,
    database,
    neighbour_ids,
    live_counts,
    entry_rows,
    enc_gain,
    enc_qkv,
    enc_out,
    final_gain,
    kv_weight,
):
    shards = lax.axis_size("db")
    per_shard = database.shape[1]
    wanted = neighbour_ids.reshape(-1)
    requests = wanted.shape[0]
    capacity = max(2, (requests + shards - 1) // shards)
    located = jnp.take(entry_rows, wanted)
    holder = located // per_shard
    within = located % per_shard
    ordinal = jnp.arange(requests)
    before = (holder[:, None] == holder[None, :]) & (ordinal[None, :] < ordinal[:, None])
    standing = jnp.sum(before.astype(jnp.int32), axis=1)
    target = holder * capacity + standing
    buckets = jnp.arange(shards * capacity)
    matched = (target[None, :] == buckets[:, None]).astype(jnp.int32)
    outgoing = jnp.sum(matched * within[None, :], axis=1).reshape(shards, capacity)
    indices = lax.all_to_all(outgoing, "db", split_axis=0, concat_axis=0, tiled=True)
    amount = indices.shape[1]
    picked = jnp.take(database, indices.reshape(-1), axis=1)
    picked = picked.reshape(database.shape[0], shards, amount, database.shape[2])
    fetched = lax.all_to_all(
        lax.all_to_all(picked, "db", split_axis=1, concat_axis=1, tiled=True),
        ("mp", "section"),
        split_axis=0,
        concat_axis=3,
        tiled=True,
    )
    fetched = fetched.reshape(fetched.shape[0], shards * capacity, fetched.shape[3])
    hidden = jnp.take(fetched, target, axis=1).astype(jnp.float32)
    my_index = lax.axis_index(("mp", "section"))
    head_size = enc_qkv.shape[3]
    score_scale = 3.0 / math.sqrt(head_size)
    for layer_index in range(enc_qkv.shape[0]):
        normed = (unit_heads(hidden) * enc_gain[layer_index]).astype(jnp.bfloat16)
        weight = enc_qkv[layer_index]

        def project(shard_rows, offset, weight=weight):
            mixture = jnp.einsum(
                "pre,eta->prta", shard_rows, weight, preferred_element_type=jnp.float32
            )
            return jnp.concatenate(
                [unit_heads(mixture[:, :, :2]), mixture[:, :, 2:]], axis=2
            ).astype(jnp.bfloat16)

        triples = gather_rows(normed, project)
        scores = (
            jnp.einsum(
                "pra,sra->rps",
                triples[:, :, 0],
                triples[:, :, 1],
                preferred_element_type=jnp.float32,
            )
            * score_scale
        )
        weights = jnp.exp(scores)
        shares = (weights / jnp.sum(weights, axis=2, keepdims=True)).astype(jnp.bfloat16)
        attended = jnp.einsum(
            "rps,sra->pra", shares, triples[:, :, 2], preferred_element_type=jnp.float32
        ).astype(jnp.bfloat16)
        rows_out = lax.dynamic_slice_in_dim(
            enc_out[layer_index], my_index * head_size, head_size, 0
        )

        def partial_term(first_row, row_count, attended=attended, rows_out=rows_out):
            return jnp.einsum("pra,ae->pre", attended, rows_out, preferred_element_type=jnp.float32)

        hidden = hidden + lax.psum_scatter(
            partial_term(jnp.int32(0), hidden.shape[0] * lax.axis_size(("mp", "section"))),
            ("mp", "section"),
            scatter_dimension=0,
            tiled=True,
        )
    encoded = (unit_heads(hidden) * final_gain).astype(jnp.bfloat16)
    heads_local = kv_weight.shape[2] // head_size

    def keys_values(shard_rows, offset):
        mixture = jnp.einsum(
            "pre,etd->prtd", shard_rows, kv_weight, preferred_element_type=jnp.float32
        )
        shaped = mixture.reshape(mixture.shape[0], mixture.shape[1], 2, heads_local, head_size)
        return jnp.concatenate([unit_heads(shaped[:, :, :1]), shaped[:, :, 1:]], axis=2).astype(
            jnp.bfloat16
        )

    key_values = gather_rows(encoded, keys_values)
    positions = key_values.shape[0]
    tokens, features = queries.shape
    block_total = live_counts.shape[0]
    neighbours = neighbour_ids.shape[1]
    query_heads = unit_heads(
        queries.reshape(tokens, heads_local, head_size).astype(jnp.float32)
    ).astype(jnp.bfloat16)
    padding = jnp.zeros((BL - 1, heads_local, head_size), jnp.bfloat16)
    shifted = jnp.concatenate([query_heads[BL - 1 :], padding], axis=0).reshape(
        block_total, BL, heads_local, head_size
    )
    key_heads = key_values[:, :, 0].reshape(
        positions, block_total, neighbours, heads_local, head_size
    )
    value_heads = key_values[:, :, 1].reshape(
        positions, block_total, neighbours, heads_local, head_size
    )
    scores = (
        jnp.einsum("cqha,scnha->chqsn", shifted, key_heads, preferred_element_type=jnp.float32)
        * score_scale
    )
    live_mask = (jnp.arange(neighbours)[None, :] < live_counts[:, None]).astype(jnp.float32)
    weights = jnp.exp(scores) * live_mask[:, None, None, None, :]
    shares = (weights / jnp.sum(weights, axis=(3, 4), keepdims=True)).astype(jnp.bfloat16)
    mixture = jnp.einsum(
        "chqsn,scnha->cqha", shares, value_heads, preferred_element_type=jnp.float32
    ).reshape(tokens, features)
    front = jnp.zeros((BL - 1, features), jnp.float32)
    return jnp.concatenate([front, mixture[: tokens - BL + 1]], axis=0).astype(jnp.bfloat16)


def solution(mesh):
    return jax.shard_map(
        on_device,
        mesh=mesh,
        in_specs=(
            P("db", ("mp", "section")),
            P(None, "db", ("mp", "section")),
            P("db", None),
            P("db"),
            P(),
            P(),
            P(None, None, None, ("mp", "section")),
            P(),
            P(),
            P(None, None, ("mp", "section")),
        ),
        out_specs=P("db", ("mp", "section")),
        check_vma=False,
    )
```

profile of v0, /device:TPU:1, one launch (start us, length us, event | category | flops | bytes accessed | tf_op | source)
XLA Modules:
  0.0 441.7 jit_solution(10445819414489083536)
XLA Ops:
  9.3 20.3 %all_to_all.29 = s32[32,1,2]{2,1,0:T(1,128)S(1)} all-to-all(s32[32,1,2]{2,1,0:T(1,128)S(1)} %bitcast.163), channel_id=1, replica_groups=mesh['db'=32,'mp'=4,'section'=2] {'db'}, dimensions={0} | all-to-all | bytes 512 | tf_op jit(solution)/shard_map/all_to_all | solution.py:46
  31.2 8.7 %gather_fusion.1 = bf16[64,128,128]{2,0,1:T(8,128)(2,1)S(1)} fusion(bf16[128,32,128]{2,1,0:T(8,128)(2,1)S(1)} %copy-done, s32[1024]{0:T(1024)S(1)} %pad_clamp_fusion.1), kind=kCustom, calls=%fused_computation.1 | custom fusion | bytes 4194560 | tf_op jit(solution)/shard_map/jit(_take)/gather | solution.py:48
  39.9 2.2 broadcast_select_fusion
  42.0 50.4 %all_to_all.30 = bf16[128,32,2,128]{3,2,0,1:T(2,128)(2,1)S(1)} all-to-all(bf16[128,32,2,128]{3,2,0,1:T(2,128)(2,1)S(1)} %broadcast_select_fusion), channel_id=1, replica_groups=mesh['db'=32,'mp'=4,'section'=2] {'db'}, dimensions={1} | all-to-all | bytes 4194304 | tf_op jit(solution)/shard_map/all_to_all | solution.py:51
  92.4 3.8 copy.149
  96.2 9.7 %all-to-all-start.2 = ((bf16[128,32,2,128]{3,1,2,0:T(8,128)(2,1)}), bf16[128,32,2,128]{3,1,2,0:T(8,128)(2,1)S(1)}, u32[]{:S(2)}, u32[]{:S(2)}) async-start(bf16[128,32,2,128]{3,1,2,0:T(8,128)(2,1)} %copy.149), calls=%async_computation.2 | async-start | bytes 4194304 | tf_op jit(solution)/shard_map/all_to_all | solution.py:50
  106.0 26.3 %all-to-all-done.2 = bf16[128,32,2,128]{3,1,2,0:T(8,128)(2,1)S(1)} async-done(((bf16[128,32,2,128]{3,1,2,0:T(8,128)(2,1)}), bf16[128,32,2,128]{3,1,2,0:T(8,128)(2,1)S(1)}, u32[]{:S(2)}, u32[]{:S(2)}) %all-to-all-start.2) | async-done | bytes 2097184 | tf_op jit(solution)/shard_map/all_to_all | solution.py:50
  132.2 2.7 copy.186
  135.0 2.8 reshape.409
  139.8 4.1 fusion.67
  143.9 25.9 %all-gather.4.cloned.1.call-done = bf16[128,16,1024]{2,0,1:T(8,128)(2,1)} async-done(((bf16[16,16,1024]{2,0,1:T(8,128)(2,1)}), bf16[128,16,1024]{2,0,1:T(8,128)(2,1)}) %all-gather.4.cloned.1.call-update) | async-done | bytes 4194320 | tf_op jit(solution)/shard_map/all_gather | solution.py:16
  169.8 3.8 fusion.4
  173.8 1.5 copy-done.6
  177.0 6.6 %fusion.27 = f32[128,16,1024]{2,0,1:T(8,128)} fusion(f32[16,128,128]{1,2,0:T(8,128)} %fusion.23, f32[128,16,3,128]{0,3,2,1:T(8,128)} %copy-done.6, bf16[1,1024,1024]{2,1,0:T(8,128)(2,1)} %get-tuple-element.10, s32[]{:T(128)S(6)} %select_n.157), kind=kOutput, calls=%fused_computation.44 | convolution fusion | flops 604768384 | bytes 11272196 | tf_op jit(solution)/shard_map/pra,ae->pre/dot_general | solution.py:94
  183.7 54.1 %reduce-scatter.3.cloned.1.call-done = f32[16,16,1024]{2,0,1:T(8,128)} async-done(((f32[128,16,1024]{2,0,1:T(8,128)}), f32[16,16,1024]{2,0,1:T(8,128)}) %reduce-scatter.3.cloned.1.call-update) | async-done | bytes 1048592 | tf_op jit(solution)/shard_map/reduce_scatter | solution.py:96
  239.3 2.3 multiply_convert_fusion.4
  241.6 35.4 %all-gather.6.cloned.1.call-done = bf16[128,16,1024]{2,0,1:T(8,128)(2,1)} async-done(((bf16[16,16,1024]{2,0,1:T(8,128)(2,1)}), bf16[128,16,1024]{2,0,1:T(8,128)(2,1)}) %all-gather.6.cloned.1.call-update) | async-done | bytes 4194320 | tf_op jit(solution)/shard_map/all_gather | solution.py:16
  277.0 3.8 fusion.2
  281.1 1.5 copy-done.5
  284.2 6.6 %fusion.26 = f32[128,16,1024]{2,0,1:T(8,128)} fusion(f32[16,128,128]{1,2,0:T(8,128)} %fusion.22, f32[128,16,3,128]{0,3,2,1:T(8,128)} %copy-done.5, bf16[1,1024,1024]{2,1,0:T(8,128)(2,1)S(1)} %get-tuple-element.9, s32[]{:T(128)S(6)} %select_n.157), kind=kOutput, calls=%fused_computation.43 | convolution fusion | flops 604768384 | bytes 11272196 | tf_op jit(solution)/shard_map/pra,ae->pre/dot_general | solution.py:94
  290.9 54.1 %reduce-scatter.5.cloned.1.call-done = f32[16,16,1024]{2,0,1:T(8,128)} async-done(((f32[128,16,1024]{2,0,1:T(8,128)}), f32[16,16,1024]{2,0,1:T(8,128)}) %reduce-scatter.5.cloned.1.call-update) | async-done | bytes 1048592 | tf_op jit(solution)/shard_map/reduce_scatter | solution.py:96
  344.9 1.6 multiply_reduce_fusion.4
  346.5 2.3 multiply_convert_fusion.3
  351.3 33.1 %all-gather.8.cloned.1.call-done = bf16[128,16,1024]{2,0,1:T(8,128)(2,1)} async-done(((bf16[16,16,1024]{2,0,1:T(8,128)(2,1)}), bf16[128,16,1024]{2,0,1:T(8,128)(2,1)}) %all-gather.8.cloned.1.call-update) | async-done | bytes 4194320 | tf_op jit(solution)/shard_map/all_gather | solution.py:16
  384.3 15.6 %fusion = f32[128,16,2,1024]{3,0,2,1:T(8,128)} fusion(bf16[128,16,1024]{2,0,1:T(8,128)(2,1)} %all-gather.8.cloned.1.call-done, bf16[1024,2,1024]{2,1,0:T(2,128)(2,1)} %param.19), kind=kOutput, calls=%fused_computation.6 | convolution fusion | flops 8589934592 | bytes 25165824 | tf_op jit(solution)/shard_map/pre,etd->prtd/dot_general | solution.py:106
  400.0 9.4 %copy.195 = f32[512,8,8,128]{3,2,1,0:T(8,128)S(1)} copy(f32[512,8,8,128]{3,1,2,0:T(8,128)} %bitcast.155) | data formatting | bytes 33554432
  409.4 2.4 multiply_reduce_fusion
  411.8 3.3 copy-done.2
  415.1 2.7 slice.104
  418.7 6.4 %multiply_convert_fusion = bf16[128,16,1,8,128]{4,3,1,0,2:T(8,128)(2,1)S(1)} fusion(f32[128,16,8]{2,1,0:T(8,128)S(1)} %copy.168, f32[128,16,2,8,128]{4,3,0,2,1:T(8,128)} %bitcast.152), kind=kLoop, calls=%fused_computation.4 | loop fusion | flops 4194304 | bytes 12648448 | tf_op jit(solution)/shard_map/slice | solution.py:126
  426.4 3.4 fusion.12
  429.8 2.8 fusion.19
  (85 shorter events, 18.3 us)
Async XLA Ops:
  6.5 24.6 %copy-start = (bf16[128,32,128]{2,1,0:T(8,128)(2,1)S(1)}, bf16[128,32,128]{2,1,0:T(8,128)(2,1)}, u32[]{:S(2)}) copy-start(bf16[128,32,128]{2,1,0:T(8,128)(2,1)} %param.11) | copy-start | bytes 3145732
  92.4 13.6 %copy-start.8 = (f32[2,1024]{1,0:T(2,128)S(1)}, f32[2,1024]{1,0:T(2,128)}, u32[]{:S(2)}) copy-start(f32[2,1024]{1,0:T(2,128)} %param.15) | copy-start | bytes 24580
  96.2 36.1 %all-to-all-start.2 = ((bf16[128,32,2,128]{3,1,2,0:T(8,128)(2,1)}), bf16[128,32,2,128]{3,1,2,0:T(8,128)(2,1)S(1)}, u32[]{:S(2)}, u32[]{:S(2)}) async-start(bf16[128,32,2,128]{3,1,2,0:T(8,128)(2,1)} %copy.149), calls=%async_computation.2 | async-start | bytes 4194304 | tf_op jit(solution)/shard_map/all_to_all | solution.py:50
  105.9 63.9 %all-gather.4.cloned.1.call-start = ((), (), s32[]{:S(2)}) async-start(), calls=%async_computation.5 | async-start | bytes 4718592 | tf_op jit(solution)/shard_map/all_gather | solution.py:16
  139.7 98.0 %reduce-scatter.3.cloned.1.call-start = ((), (), s32[]{:S(2)}) async-start(), calls=%async_computation.6 | async-start | bytes 9437184 | tf_op jit(solution)/shard_map/reduce_scatter | solution.py:96
  173.6 1.8 copy-start.6
  183.6 93.4 %all-gather.6.cloned.1.call-start = ((), (), s32[]{:S(2)}) async-start(), calls=%async_computation.7 | async-start | bytes 4718592 | tf_op jit(solution)/shard_map/all_gather | solution.py:16
  241.6 103.3 %reduce-scatter.5.cloned.1.call-start = ((), (), s32[]{:S(2)}) async-start(), calls=%async_computation.8 | async-start | bytes 9437184 | tf_op jit(solution)/shard_map/reduce_scatter | solution.py:96
  280.9 1.8 copy-start.5
  290.8 54.1 %copy-start.4 = (f32[16,16,1024]{2,0,1:T(8,128)S(1)}, f32[16,16,1024]{2,0,1:T(8,128)}, u32[]{:S(2)}) copy-start(f32[16,16,1024]{2,0,1:T(8,128)} %reduce-scatter.3.cloned.1.call-done) | copy-start | bytes 3145732
  290.8 55.7 %copy-start.9 = (f32[1024]{0:T(1024)S(1)}, f32[1024]{0:T(1024)}, u32[]{:S(2)}) copy-start(f32[1024]{0:T(1024)} %param.18) | copy-start | bytes 12292
  290.8 58.1 %copy-start.7 = (bf16[512,1024]{1,0:T(8,128)(2,1)S(1)}, bf16[512,1024]{1,0:T(8,128)(2,1)}, u32[]{:S(2)}) copy-start(bf16[512,1024]{1,0:T(8,128)(2,1)} %param.10) | copy-start | bytes 3145732
  290.8 93.5 %all-gather.8.cloned.1.call-start = ((), (), s32[]{:S(2)}) async-start(), calls=%async_computation.9 | async-start | bytes 4718592 | tf_op jit(solution)/shard_map/all_gather | solution.py:16
  349.6 1.6 copy-start.10
  409.4 5.7 %copy-start.2 = (f32[512,8,8,128]{3,2,1,0:T(8,128)}, f32[512,8,8,128]{3,2,1,0:T(8,128)S(1)}, u32[]{:S(2)}) copy-start(f32[512,8,8,128]{3,2,1,0:T(8,128)S(1)} %copy.195) | copy-start | bytes 50331652
  418.7 6.5 %copy-start.3 = (bf16[128,16,1,8,128]{4,3,0,2,1:T(8,128)(2,1)S(1)}, bf16[128,16,1,8,128]{4,3,0,2,1:T(8,128)(2,1)}, u32[]{:S(2)}) copy-start(bf16[128,16,1,8,128]{4,3,0,2,1:T(8,128)(2,1)} %slice.104) | copy-start | bytes 12582916
  429.8 5.1 %copy-start.1 = (bf16[128,32,128]{2,1,0:T(8,128)(2,1)S(1)}, bf16[128,32,128]{2,1,0:T(8,128)(2,1)}, u32[]{:S(2)}) copy-start(bf16[128,32,128]{2,1,0:T(8,128)(2,1)} %param.11) | copy-start | bytes 3145732
Sparse Core Ops, SparseCore 0:
  139.8 29.9 all-gather.3
  183.7 53.9 reduce-scatter.2
  241.7 35.2 all-gather.5
  290.9 53.9 reduce-scatter.4
  349.0 35.3 all-gather.7
where the time goes:
time: 450 us; the launch traced here: 442 us
  waiting for transfers between devices  229 us (51%)
  blocking collectives  70.7 us (16%)
  local copies, waits for them, and re-layouts  49.6 us (11%)
  matrix products  45.4 us (10%)
  other arithmetic  23.5 us (5%)
  between operations  13.8 us (3%)
  starting transfers between devices  9.91 us (2%)
    reduce_scatter x2, waiting for transfers between devices, on_device(): lax.psum_scatter(partial_term(jnp.int32(0), hidden.shape[0] * lax.axis_si...  108 us
    all_gather x3, waiting for transfers between devices, gather_rows(): lax.all_gather(tensor, ('mp', 'section'), axis=0, tiled=True)  94.4 us
    all_to_all x1, blocking collectives, on_device(): lax.all_to_all(picked, 'db', split_axis=1, concat_axis=1, tiled=True)  50.4 us
    all_to_all x1, waiting for transfers between devices, on_device(): lax.all_to_all(lax.all_to_all(picked, 'db', split_axis=1, concat_axis=1,...  26.3 us
    all_to_all x1, blocking collectives, on_device(): lax.all_to_all(outgoing, 'db', split_axis=0, concat_axis=0, tiled=True)  20.3 us
    unnamed x28, local copies, waits for them, and re-layouts  18.7 us
    dot_general x1, matrix products, keys_values(): jnp.einsum('pre,etd->prtd', shard_rows, kv_weight, preferred_element_type...  15.6 us
    dot_general x2, matrix products, partial_term(): jnp.einsum('pra,ae->pre', attended, rows_out, preferred_element_type=jnp....  13.2 us
  transfers between devices with their start and end apart: 6, of which 6 were waited for; matrix products, arithmetic and copies ran while one was open for 1% of the time, Pallas kernels for 0%

commit v1 on v0

v1 whole, which is shorter than its diff:
```python
import math

import jax
import jax.numpy as jnp
from jax import lax
from jax.sharding import PartitionSpec as P

BL = 64
GROUP = ("mp", "section")


def unit_heads(tensor):
    return tensor * lax.rsqrt(jnp.mean(tensor * tensor, axis=-1, keepdims=True) + 1e-06)


def on_device(
    queries,
    database,
    neighbour_ids,
    live_counts,
    entry_rows,
    enc_gain,
    enc_qkv,
    enc_out,
    final_gain,
    kv_weight,
):
    shards = lax.axis_size("db")
    per_shard = database.shape[1]
    head_size = enc_qkv.shape[3]
    score_scale = 3.0 / math.sqrt(head_size)
    weights_all = lax.all_gather(enc_qkv, GROUP, axis=0, tiled=False)
    wanted = neighbour_ids.reshape(-1)
    requests = wanted.shape[0]
    capacity = max(2, (requests + shards - 1) // shards)
    located = jnp.take(entry_rows, wanted)
    holder = located // per_shard
    within = located % per_shard
    ordinal = jnp.arange(requests)
    before = (holder[:, None] == holder[None, :]) & (ordinal[None, :] < ordinal[:, None])
    standing = jnp.sum(before.astype(jnp.int32), axis=1)
    target = holder * capacity + standing
    buckets = jnp.arange(shards * capacity)
    matched = (target[None, :] == buckets[:, None]).astype(jnp.int32)
    outgoing = jnp.sum(matched * within[None, :], axis=1).reshape(shards, capacity)
    indices = lax.all_to_all(outgoing, "db", split_axis=0, concat_axis=0, tiled=True)
    by_row = database.transpose(1, 0, 2)
    picked = by_row[indices.reshape(-1)]
    fetched = lax.all_to_all(picked, "db", split_axis=0, concat_axis=0, tiled=True)
    rows = fetched[target]
    mine = lax.all_to_all(rows, GROUP, split_axis=0, concat_axis=2, tiled=True)
    hidden = mine.astype(jnp.float32)
    for layer_index in range(enc_qkv.shape[0]):
        normed = (unit_heads(hidden) * enc_gain[layer_index]).astype(jnp.bfloat16)
        mixture = jnp.einsum(
            "rpe,heta->trhpa", normed, weights_all[:, layer_index], preferred_element_type=jnp.float32
        )
        query = unit_heads(mixture[0]).astype(jnp.bfloat16)
        key = unit_heads(mixture[1]).astype(jnp.bfloat16)
        value = mixture[2].astype(jnp.bfloat16)
        scores = (
            jnp.einsum("rhpa,rhsa->rhps", query, key, preferred_element_type=jnp.float32)
            * score_scale
        )
        weights = jnp.exp(scores)
        shares = (weights / jnp.sum(weights, axis=3, keepdims=True)).astype(jnp.bfloat16)
        attended = jnp.einsum(
            "rhps,rhsa->rpha", shares, value, preferred_element_type=jnp.float32
        ).astype(jnp.bfloat16)
        hidden = hidden + jnp.einsum(
            "rpf,fe->rpe",
            attended.reshape(hidden.shape),
            enc_out[layer_index],
            preferred_element_type=jnp.float32,
        )
    encoded = (unit_heads(hidden) * final_gain).astype(jnp.bfloat16)
    gathered = lax.all_gather(encoded, GROUP, axis=0, tiled=True)
    heads_local = kv_weight.shape[2] // head_size
    tokens, features = queries.shape
    block_total = live_counts.shape[0]
    neighbours = neighbour_ids.shape[1]
    positions = gathered.shape[1]
    flat = gathered.reshape(block_total, neighbours * positions, gathered.shape[2])
    weight_heads = kv_weight.reshape(kv_weight.shape[0], 2, heads_local, head_size)
    mixture = jnp.einsum(
        "cse,ethd->tchsd", flat, weight_heads, preferred_element_type=jnp.float32
    )
    key_heads = unit_heads(mixture[0]).astype(jnp.bfloat16)
    value_heads = mixture[1].astype(jnp.bfloat16)
    query_heads = unit_heads(
        queries.reshape(tokens, heads_local, head_size).astype(jnp.float32)
    ).astype(jnp.bfloat16)
    padding = jnp.zeros((BL - 1, heads_local, head_size), jnp.bfloat16)
    shifted = (
        jnp.concatenate([query_heads[BL - 1 :], padding], axis=0)
        .reshape(block_total, BL, heads_local, head_size)
        .transpose(0, 2, 1, 3)
    )
    scores = (
        jnp.einsum("chqa,chsa->chqs", shifted, key_heads, preferred_element_type=jnp.float32)
        * score_scale
    )
    slot = jnp.arange(neighbours * positions) // positions
    live_mask = (slot[None, :] < live_counts[:, None]).astype(jnp.float32)
    weights = jnp.exp(scores) * live_mask[:, None, None, :]
    shares = (weights / jnp.sum(weights, axis=3, keepdims=True)).astype(jnp.bfloat16)
    mixture = jnp.einsum(
        "chqs,chsa->cqha", shares, value_heads, preferred_element_type=jnp.float32
    ).reshape(tokens, features)
    front = jnp.zeros((BL - 1, features), jnp.float32)
    return jnp.concatenate([front, mixture[: tokens - BL + 1]], axis=0).astype(jnp.bfloat16)


def solution(mesh):
    return jax.shard_map(
        on_device,
        mesh=mesh,
        in_specs=(
            P("db", GROUP),
            P(None, "db", GROUP),
            P("db", None),
            P("db"),
            P(),
            P(),
            P(None, None, None, GROUP),
            P(),
            P(),
            P(None, None, GROUP),
        ),
        out_specs=P("db", GROUP),
        check_vma=False,
    )
```

time: 450 us -> 196 us (0.44); the launches traced: 442 us -> 195 us
  waiting for transfers between devices: 229 us -> 83.7 us
  blocking collectives: 70.7 us -> 0 us
  local copies, waits for them, and re-layouts: 49.6 us -> 25.7 us
  other arithmetic: 23.5 us -> 5.63 us
  starting transfers between devices: 9.91 us -> 22.4 us
    reduce_scatter x2 -> x0, waiting for transfers between devices: 108 us -> none  [on_device(): lax.psum_scatter(partial_term(jnp.int32(0), hidden.shape[0] * lax.axis_si...]
    all_gather x3 -> x2, waiting for transfers between devices: 94.4 us -> 17.2 us  [the longest x1 17.2 us: on_device(): gathered = lax.all_gather(encoded, GROUP, axis=0, tiled=True)]
    all_to_all x2 -> x0, blocking collectives: 70.7 us -> none  [the longest x1 50.4 us: on_device(): lax.all_to_all(picked, 'db', split_axis=1, concat_axis=1, tiled=True)]
    all_to_all x1 -> x3, waiting for transfers between devices: 26.3 us -> 65.7 us  [the longest x1 49.3 us: on_device(): lax.all_to_all(picked, 'db', split_axis=0, concat_axis=0, tiled=True)]
    unnamed x28 -> x19, local copies, waits for them, and re-layouts: 18.7 us -> 3.29 us
    all_to_all x1 -> x3, starting transfers between devices: 9.74 us -> 22.4 us  [the longest x1 11.9 us: on_device(): lax.all_to_all(outgoing, 'db', split_axis=0, concat_axis=0, tiled=True)]
    slice x2 -> x0, local copies, waits for them, and re-layouts: 6.77 us -> none  [the longest x1 4.09 us: on_device(): enc_out[layer_index]]
    slice x1 -> x0, other arithmetic: 6.45 us -> none  [on_device(): key_values[:, :, 0]]
  transfers between devices with their start and end apart: 6 -> 5, of which waited for: 6 -> 4; matrix products, arithmetic and copies ran while one was open for 1% -> 13% of each run, Pallas kernels for 0% -> 0%
where the time goes in v1:
time: 196 us; the launch traced here: 195 us
  waiting for transfers between devices  83.7 us (43%)
  matrix products  44 us (22%)
  local copies, waits for them, and re-layouts  25.7 us (13%)
  starting transfers between devices  22.4 us (11%)
  between operations  13.8 us (7%)
  other arithmetic  5.63 us (3%)
    all_to_all x1, waiting for transfers between devices, on_device(): lax.all_to_all(picked, 'db', split_axis=0, concat_axis=0, tiled=True)  49.3 us
    all_gather x1, waiting for transfers between devices, on_device(): gathered = lax.all_gather(encoded, GROUP, axis=0, tiled=True)  17.2 us
    dot_general x1, matrix products, on_device(): jnp.einsum('cse,ethd->tchsd', flat, weight_heads, preferred_element_type=...  12.2 us
    all_to_all x1, starting transfers between devices, on_device(): lax.all_to_all(outgoing, 'db', split_axis=0, concat_axis=0, tiled=True)  11.9 us
    reshape x1, local copies, waits for them, and re-layouts, on_device(): kv_weight.reshape(kv_weight.shape[0], 2, heads_local, head_size)  11.3 us
    dot_general x2, matrix products, on_device(): jnp.einsum('rpe,heta->trhpa', normed, weights_all[:, layer_index], prefer...  10.1 us
    all_to_all x1, waiting for transfers between devices, on_device(): mine = lax.all_to_all(rows, GROUP, split_axis=0, concat_axis=2, tiled=True)  9.46 us
    all_to_all x1, waiting for transfers between devices, on_device(): lax.all_to_all(outgoing, 'db', split_axis=0, concat_axis=0, tiled=True)  6.93 us
  transfers between devices with their start and end apart: 5, of which 4 were waited for; matrix products, arithmetic and copies ran while one was open for 13% of the time, Pallas kernels for 0%

profile of v1, /device:TPU:1, one launch (start us, length us, event | category | flops | bytes accessed | tf_op | source)
XLA Modules:
  0.0 195.1 jit_solution(5834767601338446188)
XLA Ops:
  6.5 0.7 all-gather.6.cloned.1.call-update
  7.3 0.8 copy.112
  9.2 0.7 all_to_all.16
  9.9 11.9 %all-to-all-start = ((s32[32,1,2]{2,1,0:T(1,128)}), s32[32,1,2]{2,1,0:T(1,128)S(1)}, u32[]{:S(2)}, u32[]{:S(2)}) async-start(s32[32,1,2]{2,1,0:T(1,128)} %bitcast.2), calls=%async_computation | async-start | bytes 32768 | tf_op jit(solution)/shard_map/all_to_all | solution.py:46
  21.7 1.6 copy.164
  23.4 6.9 %all-to-all-done = s32[32,1,2]{2,1,0:T(1,128)S(1)} async-done(((s32[32,1,2]{2,1,0:T(1,128)}), s32[32,1,2]{2,1,0:T(1,128)S(1)}, u32[]{:S(2)}, u32[]{:S(2)}) %all-to-all-start) | async-done | bytes 288 | tf_op jit(solution)/shard_map/all_to_all | solution.py:46
  30.8 0.7 reduce.5
  31.6 2.2 %gather_fusion.1 = bf16[64,128,128]{2,1,0:T(8,128)(2,1)} fusion(bf16[32,128,128]{2,1,0:T(8,128)(2,1)S(1)} %bitcast.166, s32[1024]{0:T(1024)S(1)} %pad_clamp_fusion.1), kind=kCustom, calls=%fused_computation.1 | custom fusion | bytes 4194560 | tf_op jit(solution)/shard_map/gather | solution.py:48
  33.8 4.1 %all-to-all-start.1 = ((bf16[64,128,128]{2,1,0:T(8,128)(2,1)}), bf16[64,128,128]{2,1,0:T(8,128)(2,1)S(1)}, u32[]{:S(2)}, u32[]{:S(2)}) async-start(bf16[64,128,128]{2,1,0:T(8,128)(2,1)} %gather_fusion.1), calls=%async_computation.1 | async-start | bytes 4194304 | tf_op jit(solution)/shard_map/all_to_all | solution.py:49
  38.0 49.3 %all-to-all-done.1 = bf16[64,128,128]{2,1,0:T(8,128)(2,1)S(1)} async-done(((bf16[64,128,128]{2,1,0:T(8,128)(2,1)}), bf16[64,128,128]{2,1,0:T(8,128)(2,1)S(1)}, u32[]{:S(2)}, u32[]{:S(2)}) %all-to-all-start.1) | async-done | bytes 2097184 | tf_op jit(solution)/shard_map/all_to_all | solution.py:49
  87.3 1.4 gather_fusion.2
  88.7 6.4 %all-to-all-start.2 = ((bf16[16,128,128]{2,1,0:T(8,128)(2,1)}), bf16[16,128,128]{2,1,0:T(8,128)(2,1)S(1)}, u32[]{:S(2)}, u32[]{:S(2)}) async-start(bf16[16,128,128]{2,1,0:T(8,128)(2,1)} %gather_fusion.2), calls=%async_computation.2 | async-start | bytes 1048576 | tf_op jit(solution)/shard_map/all_to_all | solution.py:51
  95.1 9.5 %all-to-all-done.2 = bf16[16,128,128]{2,1,0:T(8,128)(2,1)S(1)} async-done(((bf16[16,128,128]{2,1,0:T(8,128)(2,1)}), bf16[16,128,128]{2,1,0:T(8,128)(2,1)S(1)}, u32[]{:S(2)}, u32[]{:S(2)}) %all-to-all-start.2) | async-done | bytes 524320 | tf_op jit(solution)/shard_map/all_to_all | solution.py:51
  105.4 1.0 reshape.428
  107.1 1.1 reshape.399
  108.3 4.8 %fusion.17 = f32[3,2,8,128,128]{3,4,0,2,1:T(8,128)S(1)} fusion(bf16[8,2,1024,3,128]{4,2,3,1,0:T(8,128)(2,1)} %bitcast.177, bf16[2,128,1024,1,1]{2,1,0,3,4:T(8,128)(2,1)} %reshape.428), kind=kOutput, calls=%fused_computation.30 | convolution fusion | flops 1610612736 | bytes 9961472 | tf_op jit(solution)/shard_map/rpe,heta->trhpa/dot_general | solution.py:55
  113.3 1.4 fusion.27
  114.8 2.8 %convolution_convert_fusion.1 = bf16[2,8,128,128]{3,2,1,0:T(8,128)(2,1)} fusion(f32[2,8,128,128]{2,3,1,0:T(8,128)} %fusion.27, f32[3,2,8,128,128]{3,4,0,2,1:T(8,128)S(1)} %fusion.17), kind=kOutput, calls=%fused_computation.43 | convolution fusion | flops 67897472 | bytes 3145728 | tf_op jit(solution)/shard_map/rhps,rhsa->rpha/dot_general | solution.py:67
  117.6 2.8 %multiply_reduce_fusion.5 = (f32[2,128]{1,0:T(2,128)S(1)}, f32[2,128,1024]{2,1,0:T(8,128)S(1)}) fusion(f32[2,128,1024]{2,1,0:T(8,128)} %reshape.399, bf16[2,128,1024]{1,2,0:T(8,128)(2,1)} %bitcast.173, bf16[2,1024,1024]{2,1,0:T(8,128)(2,1)} %param.17), kind=kOutput, calls=%fused_computation.63 | convolution fusion | flops 537657088 | bytes 4719616 | tf_op jit(solution)/shard_map/rpf,fe->rpe/dot_general | solution.py:70
  120.4 5.3 %fusion.18 = f32[3,2,8,128,128]{3,4,0,2,1:T(8,128)S(1)} fusion(bf16[8,2,1024,3,128]{4,2,3,1,0:T(8,128)(2,1)} %bitcast.178, f32[2,128,1024]{2,1,0:T(8,128)S(1)} %get-tuple-element.14, f32[1024]{0:T(1024)S(1)} %bitcast.176, f32[2,128]{1,0:T(2,128)S(1)} %add_rsqrt_fusion.7), kind=kOutput, calls=%fused_computation.31 | convolution fusion | flops 1611399168 | bytes 10490880 | tf_op jit(solution)/shard_map/rpe,heta->trhpa/dot_general | solution.py:55
  125.9 1.4 fusion.26
  127.3 2.7 %convolution_convert_fusion = bf16[2,8,128,128]{3,2,1,0:T(8,128)(2,1)} fusion(f32[2,8,128,128]{2,3,1,0:T(8,128)} %fusion.26, f32[3,2,8,128,128]{3,4,0,2,1:T(8,128)S(1)} %fusion.18), kind=kOutput, calls=%fused_computation.42 | convolution fusion | flops 67897472 | bytes 3145728 | tf_op jit(solution)/shard_map/rhps,rhsa->rpha/dot_general | solution.py:67
  130.0 2.8 %multiply_reduce_fusion.2 = (f32[2,128]{1,0:T(2,128)S(1)}, f32[2,128,1024]{2,1,0:T(8,128)S(1)}) fusion(f32[2,128,1024]{2,1,0:T(8,128)} %copy-done.2, bf16[2,128,1024]{1,2,0:T(8,128)(2,1)} %bitcast.174, bf16[2,1024,1024]{2,1,0:T(8,128)(2,1)} %param.17), kind=kOutput, calls=%fused_computation.56 | convolution fusion | flops 537657088 | bytes 4719616 | tf_op jit(solution)/shard_map/rpf,fe->rpe/dot_general | solution.py:70
  132.9 0.9 multiply_convert_fusion.2
  133.9 11.3 %copy.147 = bf16[1024,2,1024]{0,2,1:T(8,128)(2,1)} copy(bf16[1024,2,1024]{2,1,0:T(2,128)(2,1)} %param.19) | data formatting | bytes 8388608 | tf_op jit(solution)/shard_map/reshape | solution.py:84
  147.6 17.2 %all-gather.4.cloned.1.call-done = bf16[16,128,1024]{2,1,0:T(8,128)(2,1)} async-done(((bf16[2,128,1024]{2,1,0:T(8,128)(2,1)}), bf16[16,128,1024]{2,1,0:T(8,128)(2,1)}) %all-gather.4.cloned.1.call-update) | async-done | bytes 4194320 | tf_op jit(solution)/shard_map/all_gather | solution.py:77
  164.8 12.2 %convolution_bitcast_fusion = f32[2,8,8,256,128]{3,4,2,0,1:T(8,128)S(1)} fusion(bf16[8,256,1024,1,1]{2,1,4,3,0:T(8,128)(2,1)} %bitcast.179, bf16[1024,2,8,128,1]{0,3,2,1,4:T(8,128)(2,1)} %bitcast.169), kind=kOutput, calls=%fused_computation.3 | convolution fusion | flops 8589934592 | bytes 25165824 | tf_op jit(solution)/shard_map/cse,ethd->tchsd/dot_general | solution.py:85
  177.0 1.2 multiply_reduce_fusion
  178.3 3.8 %fusion.7 = (f32[8,8,64]{2,1,0:T(8,128)}, f32[8,8,64,256]{3,2,1,0:T(8,128)}) fusion(f32[8,256]{1,0:T(8,128)S(1)} %compare_convert_fusion, f32[2,8,8,256,128]{3,4,2,0,1:T(8,128)S(1)} %convolution_bitcast_fusion, f32[8,8,256]{2,1,0:T(8,128)S(1)} %add_rsqrt_fusion, bf16[8,64,8,128]{3,2,1,0:T(8,128)(2,1)S(1)} %bitcast.168), kind=kOutput, calls=%fused_computation.18 | convolution fusion | flops 275771392 | bytes 13721600 | tf_op jit(solution)/shard_map/chqa,chsa->chqs/dot_general | solution.py:100
  182.1 3.9 %fusion.23 = bf16[8,64,8,128]{3,1,2,0:T(8,128)(2,1)S(1)} fusion(f32[8,8,64,256]{3,2,1,0:T(8,128)} %get-tuple-element.18, f32[8,8,64]{2,1,0:T(8,128)} %get-tuple-element.17, f32[8,256]{1,0:T(8,128)S(1)} %compare_convert_fusion, f32[2,8,8,256,128]{3,4,2,0,1:T(8,128)S(1)} %convolution_bitcast_fusion), kind=kOutput, calls=%fused_computation.35 | convolution fusion | flops 273154048 | bytes 9461760 | tf_op jit(solution)/shard_map/chqs,chsa->cqha/dot_general | solution.py:107
  186.0 0.7 copy.133
  187.1 1.2 concatenate.7
  (62 shorter events, 6.4 us)
Async XLA Ops:
  6.5 1.7 copy-start
  6.5 101.7 %all-gather.6.cloned.1.call-start = ((), (), s32[]{:S(2)}) async-start(), calls=%async_computation.4 | async-start | bytes 14155776 | tf_op jit(solution)/shard_map/all_gather | solution.py:32
  9.9 20.4 %all-to-all-start = ((s32[32,1,2]{2,1,0:T(1,128)}), s32[32,1,2]{2,1,0:T(1,128)S(1)}, u32[]{:S(2)}, u32[]{:S(2)}) async-start(s32[32,1,2]{2,1,0:T(1,128)} %bitcast.2), calls=%async_computation | async-start | bytes 32768 | tf_op jit(solution)/shard_map/all_to_all | solution.py:46
  33.8 61.3 %copy-start.4 = (f32[2,1024]{1,0:T(2,128)S(1)}, f32[2,1024]{1,0:T(2,128)}, u32[]{:S(2)}) copy-start(f32[2,1024]{1,0:T(2,128)} %param.15) | copy-start | bytes 24580
  33.8 53.5 %all-to-all-start.1 = ((bf16[64,128,128]{2,1,0:T(8,128)(2,1)}), bf16[64,128,128]{2,1,0:T(8,128)(2,1)S(1)}, u32[]{:S(2)}, u32[]{:S(2)}) async-start(bf16[64,128,128]{2,1,0:T(8,128)(2,1)} %gather_fusion.1), calls=%async_computation.1 | async-start | bytes 4194304 | tf_op jit(solution)/shard_map/all_to_all | solution.py:49
  88.7 15.9 %all-to-all-start.2 = ((bf16[16,128,128]{2,1,0:T(8,128)(2,1)}), bf16[16,128,128]{2,1,0:T(8,128)(2,1)S(1)}, u32[]{:S(2)}, u32[]{:S(2)}) async-start(bf16[16,128,128]{2,1,0:T(8,128)(2,1)} %gather_fusion.2), calls=%async_computation.2 | async-start | bytes 1048576 | tf_op jit(solution)/shard_map/all_to_all | solution.py:51
  95.1 69.7 %all-gather.4.cloned.1.call-start = ((), (), s32[]{:S(2)}) async-start(), calls=%async_computation.3 | async-start | bytes 4718592 | tf_op jit(solution)/shard_map/all_gather | solution.py:77
  120.4 5.3 %copy-start.2 = (f32[2,128,1024]{2,1,0:T(8,128)}, f32[2,128,1024]{2,1,0:T(8,128)S(1)}, u32[]{:S(2)}) copy-start(f32[2,128,1024]{2,1,0:T(8,128)S(1)} %get-tuple-element.14) | copy-start | bytes 3145732
  127.3 5.6 %copy-start.5 = (f32[1024]{0:T(1024)S(1)}, f32[1024]{0:T(1024)}, u32[]{:S(2)}) copy-start(f32[1024]{0:T(1024)} %param.18) | copy-start | bytes 12292
  133.9 11.3 %copy-start.3 = (bf16[512,1024]{1,0:T(8,128)(2,1)S(1)}, bf16[512,1024]{1,0:T(8,128)(2,1)}, u32[]{:S(2)}) copy-start(bf16[512,1024]{1,0:T(8,128)(2,1)} %param.10) | copy-start | bytes 3145732
  145.9 1.6 copy-start.6
  182.1 6.2 %copy-start.1 = (s32[1024]{0:T(1024)S(1)}, s32[1024]{0:T(1024)}, u32[]{:S(2)}) copy-start(s32[1024]{0:T(1024)} %param.14) | copy-start | bytes 12292
Sparse Core Ops, SparseCore 0:
  9.2 74.1 all-gather.5
  134.0 30.8 all-gather.3

commit v2 on v1

v2 whole, which is shorter than its diff:
```python
import functools
import math

import jax
import jax.numpy as jnp
from jax import lax
from jax.experimental import pallas as pl
from jax.experimental.pallas import tpu as pltpu
from jax.sharding import PartitionSpec as P

BL = 64
GROUP = ("mp", "section")
MESH = pl.DeviceIdType.MESH
VMEM = pl.BlockSpec(memory_space=pltpu.VMEM)
SMEM = pl.BlockSpec(memory_space=pltpu.SMEM)
ANY = pl.BlockSpec(memory_space=pl.ANY)


def unit(tensor):
    return tensor * lax.rsqrt(jnp.mean(tensor * tensor, axis=-1, keepdims=True) + 1e-06)


def remote(src, dst, send_sem, recv_sem, device):
    return pltpu.make_async_remote_copy(
        src_ref=src,
        dst_ref=dst,
        send_sem=send_sem,
        recv_sem=recv_sem,
        device_id=device,
        device_id_type=MESH,
    )


def fetch_kernel(
    shards,
    group,
    cap,
    ask_ref,
    target_ref,
    base_ref,
    out_ref,
    asked,
    asked_s,
    send,
    recv,
    rows,
    ask_send,
    ask_recv,
    row_send,
    row_recv,
    part_send,
    part_recv,
    local_sem,
):
    me = lax.axis_index("db")
    sections = 2
    lane = lax.axis_index("mp") * sections + lax.axis_index("section")

    def db_at(k):
        return {"db": lax.rem(me + k, shards)}

    def group_at(k):
        other = lax.rem(lane + k, group)
        return other, {"mp": other // sections, "section": lax.rem(other, sections)}

    barrier = pltpu.get_barrier_semaphore()

    def greet_db(k, carry):
        pl.semaphore_signal(barrier, inc=1, device_id=db_at(k), device_id_type=MESH)
        return carry

    def greet_group(k, carry):
        pl.semaphore_signal(barrier, inc=1, device_id=group_at(k)[1], device_id_type=MESH)
        return carry

    lax.fori_loop(1, shards, greet_db, 0)
    lax.fori_loop(1, group, greet_group, 0)
    pl.semaphore_wait(barrier, shards + group - 2)

    def ask(k):
        other = lax.rem(me + k, shards)
        return remote(ask_ref.at[other], asked.at[me], ask_send.at[k], ask_recv.at[k], db_at(k))

    def ask_start(k, carry):
        ask(k).start()
        return carry

    lax.fori_loop(1, shards, ask_start, 0)
    asked[pl.ds(me, 1)] = ask_ref[pl.ds(me, 1)]

    def ask_wait(k, carry):
        ask(k).wait()
        return carry

    lax.fori_loop(1, shards, ask_wait, 0)
    to_scalar = pltpu.make_async_copy(asked, asked_s, local_sem)
    to_scalar.start()
    to_scalar.wait()

    def give(k):
        other = lax.rem(me + k, shards)
        return remote(send.at[other], recv.at[me], row_send.at[k], row_recv.at[k], db_at(k))

    def pick(k, carry):
        other = lax.rem(me + k, shards)
        for slot in range(cap):
            send[other, slot] = base_ref[asked_s[other, 0, slot]]
        give(k).start()
        return carry

    lax.fori_loop(1, shards, pick, 0)
    for slot in range(cap):
        recv[me, slot] = base_ref[asked_s[me, 0, slot]]

    def give_wait(k, carry):
        give(k).wait()
        return carry

    lax.fori_loop(1, shards, give_wait, 0)

    per = rows.shape[1]

    def part(k):
        other, device = group_at(k)
        return remote(rows.at[other], out_ref.at[lane], part_send.at[k], part_recv.at[k], device)

    def choose(k, carry):
        other = lax.rem(lane + k, group)
        for slot in range(per):
            place = target_ref[other * per + slot]
            rows[other, slot] = recv[place // cap, lax.rem(place, cap)]
        part(k).start()
        return carry

    lax.fori_loop(1, group, choose, 0)
    for slot in range(per):
        place = target_ref[lane * per + slot]
        out_ref[lane, slot] = recv[place // cap, lax.rem(place, cap)]

    def part_wait(k, carry):
        part(k).wait()
        return carry

    lax.fori_loop(1, group, part_wait, 0)


def fetch(shards, group, cap, ask, target, base):
    per_shard, positions, width = base.shape
    per = target.shape[0] // group
    return pl.pallas_call(
        functools.partial(fetch_kernel, shards, group, cap),
        out_shape=jax.ShapeDtypeStruct((group, per, positions, width), base.dtype),
        in_specs=[VMEM, SMEM, VMEM],
        out_specs=VMEM,
        scratch_shapes=[
            pltpu.VMEM((shards, 1, 128), jnp.int32),
            pltpu.SMEM((shards, 1, 128), jnp.int32),
            pltpu.VMEM((shards, cap, positions, width), base.dtype),
            pltpu.VMEM((shards, cap, positions, width), base.dtype),
            pltpu.VMEM((group, per, positions, width), base.dtype),
            pltpu.SemaphoreType.DMA((shards,)),
            pltpu.SemaphoreType.DMA((shards,)),
            pltpu.SemaphoreType.DMA((shards,)),
            pltpu.SemaphoreType.DMA((shards,)),
            pltpu.SemaphoreType.DMA((group,)),
            pltpu.SemaphoreType.DMA((group,)),
            pltpu.SemaphoreType.DMA,
        ],
        compiler_params=pltpu.CompilerParams(
            collective_id=0, has_side_effects=True, vmem_limit_bytes=24 * 2**20
        ),
    )(ask, target, base)


def decode_kernel(
    group,
    scale,
    x_ref,
    live_ref,
    gain_ref,
    final_ref,
    query_ref,
    qkv0_hbm,
    qkv1_hbm,
    out_hbm,
    kv_hbm,
    mix_ref,
    qkv,
    wout,
    kv,
    hidden,
    normed,
    attended,
    queries,
    chunks,
    w_sem,
    o_sem,
    kv_sem,
    send_sem,
    recv_sem,
):
    sections = 2
    chips = group // sections
    y = lax.axis_index("mp")
    c = lax.axis_index("section")
    me = y * sections + c
    up, down, far = lax.rem(y + 1, chips), lax.rem(y + chips - 1, chips), lax.rem(y + 2, chips)
    to_up, to_down, to_twin = {"mp": up}, {"mp": down}, {"section": 1 - c}

    barrier = pltpu.get_barrier_semaphore()
    for device in (to_up, to_down, to_twin):
        pl.semaphore_signal(barrier, inc=1, device_id=device, device_id_type=MESH)

    layers = gain_ref.shape[0]
    head = x_ref.shape[3]
    per, positions = x_ref.shape[1], x_ref.shape[2]
    count = per * positions
    triple = 3 * head

    def weight_copy(source, layer, h):
        return pltpu.make_async_copy(
            source.at[h],
            qkv.at[layer, :, pl.ds(h * triple, triple)],
            w_sem.at[layer, h],
        )

    for h in range(group):
        weight_copy(qkv0_hbm, 0, h).start()
    out_copies = [
        pltpu.make_async_copy(out_hbm.at[layer], wout.at[layer], o_sem.at[layer])
        for layer in range(layers)
    ]
    out_copies[0].start()
    for h in range(group):
        weight_copy(qkv1_hbm, 1, h).start()
    out_copies[1].start()
    kv_copy = pltpu.make_async_copy(kv_hbm, kv, kv_sem)
    kv_copy.start()

    for source in range(group):
        for slot in range(per):
            hidden[pl.ds(slot * positions, positions), pl.ds(source * head, head)] = x_ref[
                source, slot
            ].astype(jnp.float32)

    for layer in range(layers):
        normed[...] = (unit(hidden[...]) * gain_ref[pl.ds(layer, 1)]).astype(jnp.bfloat16)
        for h in range(group):
            weight_copy((qkv0_hbm, qkv1_hbm)[layer], layer, h).wait()

        def heads(p, carry, layer=layer):
            start = pl.multiple_of(p * 2 * triple, 2 * triple)
            mixture = jnp.dot(
                normed[...],
                qkv[layer, :, pl.ds(start, 2 * triple)],
                preferred_element_type=jnp.float32,
            )
            for h in range(2):
                at = h * triple
                query = unit(mixture[:, at : at + head]).astype(jnp.bfloat16)
                key = unit(mixture[:, at + head : at + 2 * head]).astype(jnp.bfloat16)
                value = mixture[:, at + 2 * head : at + 3 * head].astype(jnp.bfloat16)
                for slot in range(per):
                    lo, hi = slot * positions, (slot + 1) * positions
                    scores = lax.dot_general(
                        query[lo:hi],
                        key[lo:hi],
                        (((1,), (1,)), ((), ())),
                        preferred_element_type=jnp.float32,
                    )
                    weights = jnp.exp(scores * scale)
                    shares = weights / jnp.sum(weights, axis=-1, keepdims=True)
                    attended[pl.ds(lo, positions), pl.ds(pl.multiple_of((p * 2 + h) * head, head), head)] = jnp.dot(
                        shares.astype(jnp.bfloat16), value[lo:hi], preferred_element_type=jnp.float32
                    ).astype(jnp.bfloat16)
            return carry

        lax.fori_loop(0, group // 2, heads, 0)
        out_copies[layer].wait()

        def project(t, carry, layer=layer):
            at = pl.multiple_of(t * 256, 256)
            hidden[:, pl.ds(at, 256)] += jnp.dot(
                attended[...], wout[layer, :, pl.ds(at, 256)], preferred_element_type=jnp.float32
            )
            return carry

        lax.fori_loop(0, hidden.shape[1] // 256, project, 0)

    chunks[me] = (unit(hidden[...]) * final_ref[...]).astype(jnp.bfloat16)
    half = count // 2
    pl.semaphore_wait(barrier, 3)

    def move(number, chunk, piece, device):
        place = chunks.at[chunk, pl.ds(piece * half, half)]
        return remote(place, place, send_sem.at[number], recv_sem.at[chunk, piece], device)

    def arrived(chunk, piece):
        place = chunks.at[chunk, pl.ds(piece * half, half)]
        remote(place, place, send_sem.at[0], recv_sem.at[chunk, piece], to_twin).wait_recv()

    sent = []

    def ship(chunk, piece, device):
        copy = move(len(sent), chunk, piece, device)
        copy.start()
        sent.append(copy)

    mine_up, mine_down, mine_far = up * sections + c, down * sections + c, far * sections + c
    twin = 1 - c
    for piece in range(2):
        ship(me, piece, to_up)
        ship(me, 1 - piece, to_down)
    ship(me, 0, to_twin)
    ship(me, 1, to_twin)

    blocks = live_ref.shape[0]
    queries[...] = query_ref[...]
    heads_local = query_ref.shape[1] // head
    kv_copy.wait()
    width = kv.shape[1] // 2

    def cross(chunk):
        alive = (live_ref[chunk] > 1).astype(jnp.float32)

        def pair(p, carry):
            at = pl.multiple_of(p * 2 * head, 2 * head)
            keys = jnp.dot(
                chunks[chunk], kv[:, pl.ds(at, 2 * head)], preferred_element_type=jnp.float32
            )
            values = jnp.dot(
                chunks[chunk],
                kv[:, pl.ds(pl.multiple_of(width + at, 2 * head), 2 * head)],
                preferred_element_type=jnp.float32,
            ).astype(jnp.bfloat16)
            for h in range(2):
                lanes = pl.ds(pl.multiple_of(at + h * head, head), head)
                query = unit(queries[pl.ds(pl.multiple_of(chunk * BL, BL), BL), lanes].astype(jnp.float32))
                key = unit(keys[:, h * head : (h + 1) * head]).astype(jnp.bfloat16)
                scores = lax.dot_general(
                    query.astype(jnp.bfloat16),
                    key,
                    (((1,), (1,)), ((), ())),
                    preferred_element_type=jnp.float32,
                )
                weights = jnp.exp(scores * scale)
                first, second = weights[:, :positions], weights[:, positions:] * alive
                total = jnp.sum(first + second, axis=-1, keepdims=True)
                mixed = jnp.dot(
                    (first / total).astype(jnp.bfloat16),
                    values[:positions, h * head : (h + 1) * head],
                    preferred_element_type=jnp.float32,
                ) + jnp.dot(
                    (second / total).astype(jnp.bfloat16),
                    values[positions:, h * head : (h + 1) * head],
                    preferred_element_type=jnp.float32,
                )
                mix_ref[pl.ds(pl.multiple_of(chunk * BL, BL), BL), lanes] = mixed.astype(jnp.bfloat16)
            return carry

        lax.fori_loop(0, heads_local // 2, pair, 0)

    cross(me)
    arrived(y * sections + twin, 0)
    arrived(y * sections + twin, 1)
    cross(y * sections + twin)
    arrived(mine_down, 0)
    ship(mine_down, 0, to_up)
    ship(mine_down, 0, to_twin)
    arrived(mine_up, 1)
    ship(mine_up, 1, to_down)
    ship(mine_up, 1, to_twin)
    arrived(mine_down, 1)
    ship(mine_down, 1, to_twin)
    arrived(mine_up, 0)
    ship(mine_up, 0, to_twin)
    cross(mine_down)
    cross(mine_up)
    arrived(mine_far, 0)
    ship(mine_far, 0, to_twin)
    arrived(mine_far, 1)
    ship(mine_far, 1, to_twin)
    for place in (down, up):
        arrived(place * sections + twin, 0)
        arrived(place * sections + twin, 1)
        cross(place * sections + twin)
    cross(mine_far)
    arrived(far * sections + twin, 0)
    arrived(far * sections + twin, 1)
    cross(far * sections + twin)
    for copy in sent:
        copy.wait_send()


def decode(group, x, live, gain, final, query, qkv0, qkv1, out, kv):
    head = x.shape[3]
    features = out.shape[1]
    count = x.shape[1] * x.shape[2]
    dma = pltpu.SemaphoreType.DMA
    return pl.pallas_call(
        functools.partial(decode_kernel, group, 3.0 / math.sqrt(head)),
        out_shape=jax.ShapeDtypeStruct(query.shape, jnp.bfloat16),
        in_specs=[VMEM, SMEM, VMEM, VMEM, VMEM, ANY, ANY, ANY, ANY],
        out_specs=VMEM,
        scratch_shapes=[
            pltpu.VMEM((2, features, 3 * features), jnp.bfloat16),
            pltpu.VMEM(out.shape, jnp.bfloat16),
            pltpu.VMEM(kv.shape, jnp.bfloat16),
            pltpu.VMEM((count, features), jnp.float32),
            pltpu.VMEM((count, features), jnp.bfloat16),
            pltpu.VMEM((count, features), jnp.bfloat16),
            pltpu.VMEM(query.shape, jnp.bfloat16),
            pltpu.VMEM((group, count, features), jnp.bfloat16),
            dma((2, group)),
            dma((2,)),
            dma,
            dma((14,)),
            dma((group, 2)),
        ],
        compiler_params=pltpu.CompilerParams(
            collective_id=1, has_side_effects=True, vmem_limit_bytes=52 * 2**20
        ),
    )(x, live, gain, final, query, qkv0, qkv1, out, kv)


def on_device(
    queries,
    database,
    neighbour_ids,
    live_counts,
    entry_rows,
    enc_gain,
    enc_qkv,
    enc_out,
    final_gain,
    kv_weight,
):
    shards = lax.axis_size("db")
    group = lax.axis_size(GROUP)
    per_shard = database.shape[1]
    layers, features, _, head_size = enc_qkv.shape
    own = enc_qkv.reshape(layers, features, 3 * head_size)
    qkv0 = lax.all_gather(own[0], GROUP, axis=0, tiled=False)
    qkv1 = lax.all_gather(own[1], GROUP, axis=0, tiled=False)
    wanted = neighbour_ids.reshape(-1)
    requests = wanted.shape[0]
    capacity = max(2, (requests + shards - 1) // shards)
    located = jnp.take(entry_rows, wanted)
    holder = located // per_shard
    within = located % per_shard
    ordinal = jnp.arange(requests)
    before = (holder[:, None] == holder[None, :]) & (ordinal[None, :] < ordinal[:, None])
    standing = jnp.sum(before.astype(jnp.int32), axis=1)
    target = holder * capacity + standing
    buckets = jnp.arange(shards)[:, None] * capacity + jnp.arange(128)[None, :]
    inside = jnp.arange(128)[None, :, None] < capacity
    matched = ((target[None, None, :] == buckets[:, :, None]) & inside).astype(jnp.int32)
    outgoing = jnp.sum(matched * within[None, None, :], axis=2).reshape(shards, 1, 128)
    by_row = database.transpose(1, 0, 2)
    x = fetch(shards, group, capacity, outgoing, target, by_row)

    tokens, width = queries.shape
    shifted = jnp.concatenate(
        [queries[BL - 1 :], jnp.zeros((BL - 1, width), queries.dtype)], axis=0
    )
    kv = kv_weight.reshape(kv_weight.shape[0], -1)
    mixed = decode(
        group,
        x,
        live_counts,
        enc_gain,
        final_gain.reshape(1, -1),
        shifted,
        qkv0,
        qkv1,
        enc_out,
        kv,
    )
    front = jnp.zeros((BL - 1, width), mixed.dtype)
    return jnp.concatenate([front, mixed[: tokens - BL + 1]], axis=0)


def solution(mesh):
    return jax.shard_map(
        on_device,
        mesh=mesh,
        in_specs=(
            P("db", GROUP),
            P(None, "db", GROUP),
            P("db", None),
            P("db"),
            P(),
            P(),
            P(None, None, None, GROUP),
            P(),
            P(),
            P(None, None, GROUP),
        ),
        out_specs=P("db", GROUP),
        check_vma=False,
    )
```

time: 196 us -> 172 us (0.88)
  Pallas kernels: 0 us -> 135 us
  waiting for transfers between devices: 83.7 us -> 7.54 us
  matrix products: 44 us -> 0 us
  starting transfers between devices: 22.4 us -> 0.04 us
  local copies, waits for them, and re-layouts: 25.7 us -> 15.1 us
  other arithmetic: 5.63 us -> 0.46 us
    pallas_call x0 -> x2, Pallas kernels: none -> 135 us  [the longest x1 80 us: fetch(): pl.pallas_call(functools.partial(fetch_kernel, shards, group, cap), out_s...]
    all_to_all x3 -> x0, waiting for transfers between devices: 65.7 us -> none  [the longest x1 49.3 us: on_device(): lax.all_to_all(picked, 'db', split_axis=0, concat_axis=0, tiled=True)]
    dot_general x11 -> x0, matrix products: 44 us -> none  [the longest x1 12.2 us: on_device(): jnp.einsum('cse,ethd->tchsd', flat, weight_heads, preferred_element_type=...]
    all_to_all x3 -> x0, starting transfers between devices: 22.4 us -> none  [the longest x1 11.9 us: on_device(): lax.all_to_all(outgoing, 'db', split_axis=0, concat_axis=0, tiled=True)]
    reshape x2 -> x0, local copies, waits for them, and re-layouts: 11.4 us -> none  [the longest x1 11.3 us: on_device(): kv_weight.reshape(kv_weight.shape[0], 2, heads_local, head_size)]
    all_gather x2, waiting for transfers between devices: 17.2 us -> 7.5 us  [the longest x1 7.48 us: on_device(): qkv0 = lax.all_gather(own[0], GROUP, axis=0, tiled=False)]
    slice x3 -> x5, local copies, waits for them, and re-layouts: 0.14 us -> 5.3 us  [the longest x2 2.64 us: on_device(): qkv1 = lax.all_gather(own[1], GROUP, axis=0, tiled=False)]
    gather x2 -> x0, local copies, waits for them, and re-layouts: 3.58 us -> none  [the longest x1 2.18 us: on_device(): picked = by_row[indices.reshape(-1)]]
  transfers between devices with their start and end apart: 5 -> 2, of which waited for: 4 -> 1; matrix products, arithmetic and copies ran while one was open for 13% -> 7% of each run, Pallas kernels for 0% -> 47%
where the time goes in v2:
time: 172 us
  Pallas kernels  135 us (78%)
  local copies, waits for them, and re-layouts  15.1 us (9%)
  between operations  13.5 us (8%)
  waiting for transfers between devices  7.54 us (4%)
    pallas_call x1, Pallas kernels, fetch(): pl.pallas_call(functools.partial(fetch_kernel, shards, group, cap), out_s...  80 us
    pallas_call x1, Pallas kernels, decode(): pl.pallas_call(functools.partial(decode_kernel, group, 3.0 / math.sqrt(he...  55.1 us
    all_gather x1, waiting for transfers between devices, on_device(): qkv0 = lax.all_gather(own[0], GROUP, axis=0, tiled=False)  7.48 us
    unnamed x17, local copies, waits for them, and re-layouts  6.68 us
  transfers between devices with their start and end apart: 2, of which 1 were waited for; matrix products, arithmetic and copies ran while one was open for 7% of the time, Pallas kernels for 47%

profile of v2, /device:TPU:1, one launch (start us, length us, event | category | flops | bytes accessed | tf_op | source)
XLA Modules:
  0.0 171.8 jit_solution(5160941972629758481)
XLA Ops:
  6.5 0.0 copy-start
  6.5 1.5 fusion.2
  8.0 0.0 copy-start.5
  8.0 0.3 copy.38
  8.3 0.0 copy-start.4
  8.4 1.2 copy.36
  9.5 0.0 all-gather.5.cloned.1.call-update
  9.5 0.0 all-gather.3.cloned.1.call-start
  9.6 0.3 copy.37
  9.9 1.2 copy.34
  11.1 0.0 all-gather.3.cloned.1.call-update
  11.1 0.1 copy.30
  11.2 0.1 reshape.202
  11.3 0.1 reshape.201
  11.3 1.4 slice.18
  12.8 0.4 copy.41
  13.2 0.0 copy-start.1
  13.2 0.0 copy-start.2
  13.2 0.0 copy-start.3
  13.2 5.6 %copy.39 = bf16[128,8,2,1024]{3,1,2,0:T(8,128)(2,1)} copy(bf16[128,8,2,1024]{3,2,1,0:T(2,128)(2,1)} %bitcast.15) | data formatting | bytes 8388608
  18.8 0.6 gather_fusion
  19.5 1.1 concatenate.6.query_ref
  20.6 0.2 convert_reduce_fusion
  20.8 0.1 iota_add_fusion
  20.8 0.2 select_reduce_fusion
  21.0 80.0 %shard_map.100.x_ref = bf16[8,2,128,128]{3,2,1,0:T(8,128)(2,1)S(1)} custom-call(s32[32,1,128]{2,1,0:T(1,128)S(1)} %bitcast.12, s32[16]{0:T(128)S(1)} %multiply_add_fusion.target_ref, bf16[32,128,128]{2,1,0:T(8,128)(2,1)S(1)} %bitcast.11), custom_call_target="tpu_custom_call" | custom-call | tf_op jit(solution)/shard_map/pallas_call | solution.py:150
  101.0 0.0 all-gather.5.cloned.1.call-done.qkv1_hbm
  101.0 7.5 %all-gather.3.cloned.1.call-done.qkv0_hbm = bf16[8,1024,384]{2,1,0:T(8,128)(2,1)} async-done(((bf16[1,1024,384]{2,1,0:T(8,128)(2,1)}), bf16[8,1024,384]{2,1,0:T(8,128)(2,1)}) %all-gather.3.cloned.1.call-update) | async-done | bytes 6291472 | tf_op jit(solution)/shard_map/all_gather | solution.py:443
  108.5 0.0 copy-done.2
  108.5 55.1 %shard_map.101 = bf16[512,1024]{1,0:T(8,128)(2,1)S(1)} custom-call(bf16[8,2,128,128]{3,2,1,0:T(8,128)(2,1)S(1)} %shard_map.100.x_ref, s32[8]{0:T(128)S(1)} %copy-done.3, f32[2,1024]{1,0:T(2,128)S(1)} %copy-done.1, f32[1,1024]{1,0:T(1,128)S(1)} %bitcast.13, bf16[512,1024]{1,0:T(8,128)(2,1)} %concatenate.6.query_ref, ...), custom_call_target="tpu_custom_call" | custom-call | tf_op jit(solution)/shard_map/pallas_call | solution.py:400
  163.7 0.1 slice.23
  163.7 1.2 concatenate.7
  (13 shorter events, 0.1 us)
Async XLA Ops:
  6.5 12.3 %copy-start = (s32[1024]{0:T(1024)S(1)}, s32[1024]{0:T(1024)}, u32[]{:S(2)}) copy-start(s32[1024]{0:T(1024)} %param.14) | copy-start | bytes 12292
  6.5 94.5 %all-gather.5.cloned.1.call-start = ((), (), s32[]{:S(2)}) async-start(), calls=%async_computation.1 | async-start | bytes 7077888 | tf_op jit(solution)/shard_map/all_gather | solution.py:444
  8.0 3.1 %copy-start.5 = (s32[8,2]{0,1:T(2,128)S(1)}, s32[8,2]{0,1:T(2,128)}, u32[]{:S(2)}) copy-start(s32[8,2]{0,1:T(2,128)} %param.12) | copy-start | bytes 196
  8.3 4.4 %copy-start.4 = (bf16[128,32,128]{2,1,0:T(8,128)(2,1)S(1)}, bf16[128,32,128]{2,1,0:T(8,128)(2,1)}, u32[]{:S(2)}) copy-start(bf16[128,32,128]{2,1,0:T(8,128)(2,1)} %param.11) | copy-start | bytes 3145732
  9.5 99.0 %all-gather.3.cloned.1.call-start = ((), (), s32[]{:S(2)}) async-start(), calls=%async_computation | async-start | bytes 7077888 | tf_op jit(solution)/shard_map/all_gather | solution.py:443
  13.2 95.3 %copy-start.1 = (f32[2,1024]{1,0:T(2,128)S(1)}, f32[2,1024]{1,0:T(2,128)}, u32[]{:S(2)}) copy-start(f32[2,1024]{1,0:T(2,128)} %gain_ref.1) | copy-start | bytes 24580
  13.2 95.3 %copy-start.2 = (f32[1024]{0:T(1024)S(1)}, f32[1024]{0:T(1024)}, u32[]{:S(2)}) copy-start(f32[1024]{0:T(1024)} %param.18) | copy-start | bytes 12292
  13.2 95.3 %copy-start.3 = (s32[8]{0:T(128)S(1)}, s32[8]{0:T(128)}, u32[]{:S(2)}) copy-start(s32[8]{0:T(128)} %live_ref.1) | copy-start | bytes 100
Sparse Core Ops, SparseCore 0:
  9.7 47.7 all-gather.4
  59.3 49.1 all-gather.2

commit v3 on v1

v3 whole, which is shorter than its diff:
```python
import functools
import math

import jax
import jax.numpy as jnp
from jax import lax
from jax.experimental import pallas as pl
from jax.experimental.pallas import tpu as pltpu
from jax.sharding import PartitionSpec as P

BL = 64
GROUP = ("mp", "section")
MESH = pl.DeviceIdType.MESH
VMEM = pl.BlockSpec(memory_space=pltpu.VMEM)
SMEM = pl.BlockSpec(memory_space=pltpu.SMEM)
ANY = pl.BlockSpec(memory_space=pl.ANY)


def unit(tensor):
    return tensor * lax.rsqrt(jnp.mean(tensor * tensor, axis=-1, keepdims=True) + 1e-06)


def remote(src, dst, send_sem, recv_sem, device):
    return pltpu.make_async_remote_copy(
        src_ref=src,
        dst_ref=dst,
        send_sem=send_sem,
        recv_sem=recv_sem,
        device_id=device,
        device_id_type=MESH,
    )


def kernel(
    shards,
    group,
    cap,
    scale,
    ask_ref,
    target_ref,
    base_ref,
    live_ref,
    gain_ref,
    final_ref,
    query_ref,
    own_hbm,
    out_hbm,
    kv_hbm,
    mix_ref,
    asked,
    asked_s,
    send,
    recv,
    rows,
    parts,
    wall,
    wout,
    kv,
    hidden,
    normed,
    attended,
    stage,
    queries,
    chunks,
    ask_send,
    ask_recv,
    row_send,
    row_recv,
    part_send,
    part_recv,
    asked_sem,
    own_sem,
    out_sem,
    kv_sem,
    wall_send,
    wall_recv,
    chunk_send,
    chunk_recv,
):
    sections = 2
    chips = group // sections
    db = lax.axis_index("db")
    y = lax.axis_index("mp")
    c = lax.axis_index("section")
    me = y * sections + c
    up, down, far = lax.rem(y + 1, chips), lax.rem(y + chips - 1, chips), lax.rem(y + 2, chips)
    to_up, to_down, to_twin = {"mp": up}, {"mp": down}, {"section": 1 - c}
    at_up, at_down, at_far = up * sections + c, down * sections + c, far * sections + c
    at_twin = y * sections + 1 - c
    up_twin, down_twin, far_twin = (place * sections + 1 - c for place in (up, down, far))

    layers, features = gain_ref.shape
    positions, head = base_ref.shape[1], base_ref.shape[2]
    per = rows.shape[1]
    pair = 2 * head
    blocks = live_ref.shape[0]

    own_copies = [
        pltpu.make_async_copy(
            own_hbm.at[layer],
            wall.at[layer, :, :, pl.ds(pl.multiple_of(me * head, head), head)],
            own_sem.at[layer],
        )
        for layer in range(layers)
    ]
    out_copy = pltpu.make_async_copy(out_hbm, wout, out_sem)
    kv_copy = pltpu.make_async_copy(kv_hbm, kv, kv_sem)

    def db_at(k):
        return {"db": lax.rem(db + k, shards)}

    def group_at(k):
        other = lax.rem(me + k, group)
        return other, {"mp": other // sections, "section": lax.rem(other, sections)}

    barrier = pltpu.get_barrier_semaphore()

    def greet_db(k, carry):
        pl.semaphore_signal(barrier, inc=1, device_id=db_at(k), device_id_type=MESH)
        return carry

    def greet_group(k, carry):
        pl.semaphore_signal(barrier, inc=1, device_id=group_at(k)[1], device_id_type=MESH)
        return carry

    lax.fori_loop(1, shards, greet_db, 0)
    lax.fori_loop(1, group, greet_group, 0)
    for copy in own_copies + [out_copy, kv_copy]:
        copy.start()
    pl.semaphore_wait(barrier, shards + group - 2)

    def ask(k):
        other = lax.rem(db + k, shards)
        return remote(ask_ref.at[other], asked.at[db], ask_send.at[k], ask_recv.at[k], db_at(k))

    def ask_start(k, carry):
        ask(k).start()
        return carry

    lax.fori_loop(1, shards, ask_start, 0)
    asked[pl.ds(db, 1)] = ask_ref[pl.ds(db, 1)]

    half_rows = features // 2

    def wall_place(layer, chunk, piece):
        return wall.at[
            layer,
            :,
            pl.ds(piece * half_rows, half_rows),
            pl.ds(pl.multiple_of(chunk * head, head), head),
        ]

    def wall_ship(number, layer, chunk, piece, device, own=False):
        place = wall_place(layer, chunk, piece)
        source = own_hbm.at[layer, :, pl.ds(piece * half_rows, half_rows), :] if own else place
        copy = remote(
            source, place, wall_send.at[layer, number], wall_recv.at[layer, chunk, piece], device
        )
        copy.start()
        return copy

    def wall_arrived(layer, chunk, piece):
        place = wall_place(layer, chunk, piece)
        remote(
            place, place, wall_send.at[layer, 0], wall_recv.at[layer, chunk, piece], to_twin
        ).wait_recv()

    sent = []

    def wall_own(layer):
        for piece in range(2):
            sent.append(wall_ship(piece, layer, me, piece, to_up, True))
            sent.append(wall_ship(2 + piece, layer, me, 1 - piece, to_down, True))
        for piece in range(2):
            sent.append(wall_ship(4 + piece, layer, me, piece, to_twin, True))

    def wall_near(layer):
        wall_arrived(layer, at_down, 0)
        sent.append(wall_ship(6, layer, at_down, 0, to_up))
        sent.append(wall_ship(7, layer, at_down, 0, to_twin))
        wall_arrived(layer, at_up, 1)
        sent.append(wall_ship(8, layer, at_up, 1, to_down))
        sent.append(wall_ship(9, layer, at_up, 1, to_twin))
        wall_arrived(layer, at_down, 1)
        sent.append(wall_ship(10, layer, at_down, 1, to_twin))
        wall_arrived(layer, at_up, 0)
        sent.append(wall_ship(11, layer, at_up, 0, to_twin))

    def wall_far(layer):
        for piece in range(2):
            wall_arrived(layer, at_far, piece)
            sent.append(wall_ship(12 + piece, layer, at_far, piece, to_twin))

    def ask_wait(k, carry):
        ask(k).wait()
        return carry

    lax.fori_loop(1, shards, ask_wait, 0)
    to_scalar = pltpu.make_async_copy(asked, asked_s, asked_sem)
    to_scalar.start()
    to_scalar.wait()

    def give(k):
        other = lax.rem(db + k, shards)
        return remote(send.at[other], recv.at[db], row_send.at[k], row_recv.at[k], db_at(k))

    def pick(k, carry):
        other = lax.rem(db + k, shards)
        for slot in range(cap):
            send[other, slot] = base_ref[asked_s[other, 0, slot]]
        give(k).start()
        return carry

    lax.fori_loop(1, shards, pick, 0)
    for slot in range(cap):
        recv[db, slot] = base_ref[asked_s[db, 0, slot]]

    wall_own(0)

    heads_local = query_ref.shape[1] // head
    tokens = query_ref.shape[0]

    def prepare(h, carry):
        lanes = pl.ds(pl.multiple_of(h * head, head), head)
        stage[pl.ds(0, tokens)] = unit(query_ref[:, lanes].astype(jnp.float32)) * scale
        stage[pl.ds(tokens, BL)] = jnp.zeros((BL, head), jnp.float32)
        queries[:, lanes] = stage[pl.ds(BL - 1, tokens)].astype(jnp.bfloat16)
        return carry

    lax.fori_loop(0, heads_local, prepare, 0)

    wall_near(0)
    wall_own(1)
    wall_far(0)
    wall_near(1)
    wall_far(1)

    def give_wait(k, carry):
        give(k).wait()
        return carry

    lax.fori_loop(1, shards, give_wait, 0)

    def part(k):
        other, device = group_at(k)
        return remote(rows.at[other], parts.at[me], part_send.at[k], part_recv.at[k], device)

    def choose(k, carry):
        other = lax.rem(me + k, group)
        for slot in range(per):
            place = target_ref[other * per + slot]
            rows[other, slot] = recv[place // cap, lax.rem(place, cap)]
        part(k).start()
        return carry

    lax.fori_loop(1, group, choose, 0)
    for slot in range(per):
        place = target_ref[me * per + slot]
        parts[me, slot] = recv[place // cap, lax.rem(place, cap)]

    def part_wait(k, carry):
        part(k).wait()
        return carry

    lax.fori_loop(1, group, part_wait, 0)

    for source in range(group):
        for slot in range(per):
            hidden[pl.ds(slot * positions, positions), pl.ds(source * head, head)] = parts[
                source, slot
            ].astype(jnp.float32)

    same = lax.broadcasted_iota(jnp.int32, (pair, pair), 0) // head == (
        lax.broadcasted_iota(jnp.int32, (pair, pair), 1) // head
    )
    average = jnp.where(same, 1.0 / head, 0.0).astype(jnp.bfloat16)
    ones = jnp.ones((positions, head), jnp.bfloat16)

    def unit_pair(tensor):
        square = (tensor * tensor).astype(jnp.bfloat16)
        return tensor * lax.rsqrt(
            jnp.dot(square, average, preferred_element_type=jnp.float32) + 1e-06
        )

    def product(left, right):
        return jnp.dot(left, right, preferred_element_type=jnp.float32)

    def against(left, right):
        return lax.dot_general(
            left, right, (((1,), (1,)), ((), ())), preferred_element_type=jnp.float32
        )

    out_copy.wait()
    for layer in range(layers):
        own_copies[layer].wait()
        for chunk in (at_twin, up_twin, down_twin, far_twin):
            for piece in range(2):
                wall_arrived(layer, chunk, piece)

    def encode(layer, carry):
        normed[...] = (unit(hidden[...]) * gain_ref[pl.ds(layer, 1)]).astype(jnp.bfloat16)
        for p in range(group // 2):
            lanes = pl.ds(p * pair, pair)
            query = unit_pair(product(normed[...], wall[layer, 0, :, lanes])) * scale
            key = unit_pair(product(normed[...], wall[layer, 1, :, lanes])).astype(jnp.bfloat16)
            value = product(normed[...], wall[layer, 2, :, lanes]).astype(jnp.bfloat16)
            query = query.astype(jnp.bfloat16)
            for h in range(2):
                here = slice(h * head, (h + 1) * head)
                for slot in range(per):
                    span = slice(slot * positions, (slot + 1) * positions)
                    weights = jnp.exp2(against(query[span, here], key[span, here]))
                    mixed = product(
                        weights.astype(jnp.bfloat16),
                        jnp.concatenate([value[span, here], ones], axis=1),
                    )
                    attended[
                        pl.ds(slot * positions, positions), pl.ds(p * pair + h * head, head)
                    ] = (mixed[:, :head] / mixed[:, head:]).astype(jnp.bfloat16)
        for t in range(features // 256):
            lanes = pl.ds(t * 256, 256)
            hidden[:, lanes] += product(attended[...], wout[layer, :, lanes])
        return carry

    lax.fori_loop(0, layers, encode, 0)
    chunks[me] = (unit(hidden[...]) * final_ref[...]).astype(jnp.bfloat16)
    half = chunks.shape[1] // 2

    def ship(number, chunk, piece, device):
        place = chunks.at[chunk, pl.ds(piece * half, half)]
        remote(place, place, chunk_send.at[number], chunk_recv.at[chunk, piece], device).start()

    def arrived(chunk, piece):
        place = chunks.at[chunk, pl.ds(piece * half, half)]
        remote(
            place, place, chunk_send.at[0], chunk_recv.at[chunk, piece], to_twin
        ).wait_recv()

    for piece in range(2):
        ship(piece, me, piece, to_up)
        ship(2 + piece, me, 1 - piece, to_down)
    for piece in range(2):
        ship(4 + piece, me, piece, to_twin)
    kv_copy.wait()

    def cross(step, carry):
        @pl.when(step == 1)
        def _():
            for piece in range(2):
                arrived(at_twin, piece)

        @pl.when(step == 2)
        def _():
            arrived(at_down, 0)
            ship(6, at_down, 0, to_up)
            ship(7, at_down, 0, to_twin)
            arrived(at_up, 1)
            ship(8, at_up, 1, to_down)
            ship(9, at_up, 1, to_twin)
            arrived(at_down, 1)
            ship(10, at_down, 1, to_twin)

        @pl.when(step == 3)
        def _():
            arrived(at_up, 0)
            ship(11, at_up, 0, to_twin)

        @pl.when(step == 4)
        def _():
            for piece in range(2):
                arrived(down_twin, piece)

        @pl.when(step == 5)
        def _():
            for piece in range(2):
                arrived(up_twin, piece)

        @pl.when(step == 6)
        def _():
            for piece in range(2):
                arrived(at_far, piece)
                ship(12 + piece, at_far, piece, to_twin)

        @pl.when(step == 7)
        def _():
            for piece in range(2):
                arrived(far_twin, piece)

        chunk = at_far
        for number, place in enumerate(
            (me, at_twin, at_down, at_up, down_twin, up_twin, at_far, far_twin)
        ):
            chunk = jnp.where(step == number, place, chunk)
        alive = (live_ref[chunk] > 1).astype(jnp.float32)
        span = pl.ds(pl.multiple_of(chunk * BL, BL), BL)
        for p in range(heads_local // 2):
            lanes = pl.ds(p * pair, pair)
            key = unit_pair(product(chunks[chunk], kv[0, :, lanes])).astype(jnp.bfloat16)
            value = product(chunks[chunk], kv[1, :, lanes]).astype(jnp.bfloat16)
            for h in range(2):
                here = slice(h * head, (h + 1) * head)
                weights = jnp.exp2(
                    against(queries[span, pl.ds(p * pair + h * head, head)], key[:, here])
                )
                weights = jnp.concatenate(
                    [weights[:, :positions], weights[:, positions:] * alive], axis=1
                ).astype(jnp.bfloat16)
                mixed = product(
                    weights,
                    jnp.concatenate(
                        [value[:, here], jnp.concatenate([ones, ones], axis=0)], axis=1
                    ),
                )
                mix_ref[span, pl.ds(p * pair + h * head, head)] = (
                    mixed[:, :head] / mixed[:, head:]
                ).astype(jnp.bfloat16)
        return carry

    lax.fori_loop(0, blocks, cross, 0)
    for number in range(14):
        place = chunks.at[me, pl.ds(0, half)]
        remote(place, place, chunk_send.at[number], chunk_recv.at[me, 0], to_twin).wait_send()
    for copy in sent:
        copy.wait_send()


def retrieve(shards, group, cap, ask, target, base, live, gain, final, query, own, out, kv):
    _, positions, head = base.shape
    layers, features = gain.shape
    per = target.shape[0] // group
    tokens = query.shape[0]
    dma = pltpu.SemaphoreType.DMA
    bf16, f32 = jnp.bfloat16, jnp.float32
    return pl.pallas_call(
        functools.partial(kernel, shards, group, cap, 3.0 / math.sqrt(head) * math.log2(math.e)),
        out_shape=jax.ShapeDtypeStruct(query.shape, bf16),
        in_specs=[VMEM, SMEM, VMEM, SMEM, VMEM, VMEM, VMEM, ANY, ANY, ANY],
        out_specs=VMEM,
        scratch_shapes=[
            pltpu.VMEM((shards, 1, 128), jnp.int32),
            pltpu.SMEM((shards, 1, 128), jnp.int32),
            pltpu.VMEM((shards, cap, positions, head), bf16),
            pltpu.VMEM((shards, cap, positions, head), bf16),
            pltpu.VMEM((group, per, positions, head), bf16),
            pltpu.VMEM((group, per, positions, head), bf16),
            pltpu.VMEM((layers, 3, features, features), bf16),
            pltpu.VMEM(out.shape, bf16),
            pltpu.VMEM(kv.shape, bf16),
            pltpu.VMEM((per * positions, features), f32),
            pltpu.VMEM((per * positions, features), bf16),
            pltpu.VMEM((per * positions, features), bf16),
            pltpu.VMEM((tokens + BL, head), f32),
            pltpu.VMEM(query.shape, bf16),
            pltpu.VMEM((group, per * positions, features), bf16),
            dma((shards,)),
            dma((shards,)),
            dma((shards,)),
            dma((shards,)),
            dma((group,)),
            dma((group,)),
            dma,
            dma((layers,)),
            dma,
            dma,
            dma((layers, 14)),
            dma((layers, group, 2)),
            dma((14,)),
            dma((group, 2)),
        ],
        compiler_params=pltpu.CompilerParams(
            collective_id=0, has_side_effects=True, vmem_limit_bytes=52 * 2**20
        ),
    )(ask, target, base, live, gain, final, query, own, out, kv)


def on_device(
    queries,
    database,
    neighbour_ids,
    live_counts,
    entry_rows,
    enc_gain,
    enc_qkv,
    enc_out,
    final_gain,
    kv_weight,
):
    shards = lax.axis_size("db")
    group = lax.axis_size(GROUP)
    per_shard = database.shape[1]
    wanted = neighbour_ids.reshape(-1)
    requests = wanted.shape[0]
    capacity = max(2, (requests + shards - 1) // shards)
    located = jnp.take(entry_rows, wanted)
    holder = located // per_shard
    within = located % per_shard
    ordinal = jnp.arange(requests)
    before = (holder[:, None] == holder[None, :]) & (ordinal[None, :] < ordinal[:, None])
    standing = jnp.sum(before.astype(jnp.int32), axis=1)
    target = holder * capacity + standing
    buckets = jnp.arange(shards)[:, None] * capacity + jnp.arange(128)[None, :]
    inside = jnp.arange(128)[None, :, None] < capacity
    matched = ((target[None, None, :] == buckets[:, :, None]) & inside).astype(jnp.int32)
    outgoing = jnp.sum(matched * within[None, None, :], axis=2).reshape(shards, 1, 128)
    by_row = database.transpose(1, 0, 2)
    mixed = retrieve(
        shards,
        group,
        capacity,
        outgoing,
        target,
        by_row,
        live_counts,
        enc_gain,
        final_gain.reshape(1, -1),
        queries,
        enc_qkv.transpose(0, 2, 1, 3),
        enc_out,
        kv_weight.transpose(1, 0, 2),
    )
    tokens, width = queries.shape
    front = jnp.zeros((BL - 1, width), mixed.dtype)
    return jnp.concatenate([front, mixed[: tokens - BL + 1]], axis=0)


def solution(mesh):
    return jax.shard_map(
        on_device,
        mesh=mesh,
        in_specs=(
            P("db", GROUP),
            P(None, "db", GROUP),
            P("db", None),
            P("db"),
            P(),
            P(),
            P(None, None, None, GROUP),
            P(),
            P(),
            P(None, None, GROUP),
        ),
        out_specs=P("db", GROUP),
        check_vma=False,
    )
```

time: 196 us -> 143 us (0.73)
  Pallas kernels: 0 us -> 132 us
  waiting for transfers between devices: 83.7 us -> 0 us
  matrix products: 44 us -> 0 us
  starting transfers between devices: 22.4 us -> 0 us
  local copies, waits for them, and re-layouts: 25.7 us -> 10.9 us
  between operations: 13.8 us -> 0.06 us
  other arithmetic: 5.63 us -> 0.45 us
    pallas_call x0 -> x1, Pallas kernels: none -> 132 us  [retrieve(): pl.pallas_call(functools.partial(kernel, shards, group, cap, 3.0 / math.s...]
    all_to_all x3 -> x0, waiting for transfers between devices: 65.7 us -> none  [the longest x1 49.3 us: on_device(): lax.all_to_all(picked, 'db', split_axis=0, concat_axis=0, tiled=True)]
    dot_general x11 -> x0, matrix products: 44 us -> none  [the longest x1 12.2 us: on_device(): jnp.einsum('cse,ethd->tchsd', flat, weight_heads, preferred_element_type=...]
    all_to_all x3 -> x0, starting transfers between devices: 22.4 us -> none  [the longest x1 11.9 us: on_device(): lax.all_to_all(outgoing, 'db', split_axis=0, concat_axis=0, tiled=True)]
    all_gather x2 -> x0, waiting for transfers between devices: 17.2 us -> none  [the longest x1 17.2 us: on_device(): gathered = lax.all_gather(encoded, GROUP, axis=0, tiled=True)]
    reshape x2 -> x0, local copies, waits for them, and re-layouts: 11.4 us -> none  [the longest x1 11.3 us: on_device(): kv_weight.reshape(kv_weight.shape[0], 2, heads_local, head_size)]
    unnamed x19 -> x11, local copies, waits for them, and re-layouts: 3.29 us -> 8.85 us
    gather x2 -> x0, local copies, waits for them, and re-layouts: 3.58 us -> none  [the longest x1 2.18 us: on_device(): picked = by_row[indices.reshape(-1)]]
  transfers between devices with their start and end apart: 5 -> 0, of which waited for: 4 -> 0; matrix products, arithmetic and copies ran while one was open for 13% -> 0% of each run, Pallas kernels for 0% -> 0%
where the time goes in v3:
time: 143 us
  Pallas kernels  132 us (92%)
  local copies, waits for them, and re-layouts  10.9 us (8%)
    pallas_call x1, Pallas kernels, retrieve(): pl.pallas_call(functools.partial(kernel, shards, group, cap, 3.0 / math.s...  132 us
    unnamed x11, local copies, waits for them, and re-layouts  8.85 us

profile of v3, /device:TPU:1, one launch (start us, length us, event | category | flops | bytes accessed | tf_op | source)
XLA Modules:
  0.0 143.2 jit_solution(7791216374509814186)
XLA Ops:
  0.0 0.0 copy-start
  0.0 0.8 copy.19
  0.8 0.1 reshape.196
  0.9 0.1 reshape.195
  0.9 0.0 copy-done
  1.0 0.6 gather_fusion
  1.6 0.2 convert_reduce_fusion
  1.8 0.1 iota_add_fusion
  1.9 0.2 select_reduce_fusion
  2.1 2.6 %copy.26 = bf16[128,32,128]{2,0,1:T(8,128)(2,1)} copy(bf16[128,32,128]{2,1,0:T(8,128)(2,1)} %param.11) | data formatting | bytes 2097152 | tf_op args[1]
  4.7 0.0 copy-start.1
  4.7 0.0 copy-start.2
  4.7 0.0 copy-start.3
  4.7 5.5 %copy.25 = bf16[1024,2,1024]{2,0,1:T(8,128)(2,1)} copy(bf16[1024,2,1024]{2,1,0:T(2,128)(2,1)} %param.19) | data formatting | bytes 8388608 | tf_op args[9]
  10.1 0.0 copy-done.1
  10.1 0.0 copy-done.2
  10.1 0.0 copy-done.3
  10.2 131.8 %shard_map.100 = bf16[512,1024]{1,0:T(8,128)(2,1)S(1)} custom-call(s32[32,1,128]{2,1,0:T(1,128)S(1)} %bitcast.11, s32[16]{0:T(128)S(1)} %get-tuple-element.8.target_ref, bf16[32,128,128]{2,1,0:T(8,128)(2,1)} %bitcast.14, s32[8]{0:T(128)S(1)} %copy-done.3, f32[2,1024]{1,0:T(2,128)S(1)} %copy-done.1, f32[1,1024]{1,0:T(1,128)S(1)} %bitcast.12, ...), custom_call_target="tpu_custom_call" | custom-call | tf_op jit(solution)/shard_map/pallas_call | solution.py:434
  142.0 0.1 slice.3
  142.0 1.2 concatenate.3
  (6 shorter events, 0.0 us)
Async XLA Ops:
  0.0 1.0 copy-start
  4.7 5.5 %copy-start.1 = (f32[2,1024]{1,0:T(2,128)S(1)}, f32[2,1024]{1,0:T(2,128)}, u32[]{:S(2)}) copy-start(f32[2,1024]{1,0:T(2,128)} %gain_ref.1) | copy-start | bytes 24580
  4.7 5.5 %copy-start.2 = (f32[1024]{0:T(1024)S(1)}, f32[1024]{0:T(1024)}, u32[]{:S(2)}) copy-start(f32[1024]{0:T(1024)} %param.18) | copy-start | bytes 12292
  4.7 5.5 %copy-start.3 = (s32[8]{0:T(128)S(1)}, s32[8]{0:T(128)}, u32[]{:S(2)}) copy-start(s32[8]{0:T(128)} %live_ref.1) | copy-start | bytes 100

commit v4 on v3

--- a/solution.py
+++ b/solution.py
@@ -38,7 +38,7 @@
     scale,
     ask_ref,
     target_ref,
-    base_ref,
+    data_ref,
     live_ref,
     gain_ref,
     final_ref,
@@ -47,20 +47,27 @@
     out_hbm,
     kv_hbm,
     mix_ref,
+    base,
     asked,
     asked_s,
     send,
     recv,
     rows,
     parts,
+    own_raw,
+    own,
     wall,
     wout,
+    kv_raw,
     kv,
     hidden,
     normed,
     attended,
     stage,
     queries,
+    query_s,
+    key_s,
+    value_s,
     chunks,
     ask_send,
     ask_recv,
@@ -90,21 +97,16 @@
     up_twin, down_twin, far_twin = (place * sections + 1 - c for place in (up, down, far))
 
     layers, features = gain_ref.shape
-    positions, head = base_ref.shape[1], base_ref.shape[2]
+    positions, head = base.shape[1], base.shape[2]
     per = rows.shape[1]
     pair = 2 * head
     blocks = live_ref.shape[0]
 
-    own_copies = [
-        pltpu.make_async_copy(
-            own_hbm.at[layer],
-            wall.at[layer, :, :, pl.ds(pl.multiple_of(me * head, head), head)],
-            own_sem.at[layer],
-        )
-        for layer in range(layers)
-    ]
+    own_copy = pltpu.make_async_copy(own_hbm, own_raw, own_sem)
     out_copy = pltpu.make_async_copy(out_hbm, wout, out_sem)
-    kv_copy = pltpu.make_async_copy(kv_hbm, kv, kv_sem)
+    kv_copy = pltpu.make_async_copy(kv_hbm, kv_raw, kv_sem)
+    for copy in (own_copy, out_copy, kv_copy):
+        copy.start()
 
     def db_at(k):
         return {"db": lax.rem(db + k, shards)}
@@ -125,8 +127,12 @@
 
     lax.fori_loop(1, shards, greet_db, 0)
     lax.fori_loop(1, group, greet_group, 0)
-    for copy in own_copies + [out_copy, kv_copy]:
-        copy.start()
+    mine = pl.ds(pl.multiple_of(me * head, head), head)
+    own_copy.wait()
+    for layer in range(layers):
+        own[layer] = jnp.transpose(own_raw[layer], (1, 0, 2))
+        wall[layer, :, :, mine] = own[layer]
+    base[...] = jnp.transpose(data_ref[...], (1, 0, 2))
     pl.semaphore_wait(barrier, shards + group - 2)
 
     def ask(k):
@@ -150,9 +156,9 @@
             pl.ds(pl.multiple_of(chunk * head, head), head),
         ]
 
-    def wall_ship(number, layer, chunk, piece, device, own=False):
+    def wall_ship(number, layer, chunk, piece, device, local=False):
         place = wall_place(layer, chunk, piece)
-        source = own_hbm.at[layer, :, pl.ds(piece * half_rows, half_rows), :] if own else place
+        source = own.at[layer, :, pl.ds(piece * half_rows, half_rows), :] if local else place
         copy = remote(
             source, place, wall_send.at[layer, number], wall_recv.at[layer, chunk, piece], device
         )
@@ -191,6 +197,8 @@
             wall_arrived(layer, at_far, piece)
             sent.append(wall_ship(12 + piece, layer, at_far, piece, to_twin))
 
+    wall_own(0)
+
     def ask_wait(k, carry):
         ask(k).wait()
         return carry
@@ -207,15 +215,13 @@
     def pick(k, carry):
         other = lax.rem(db + k, shards)
         for slot in range(cap):
-            send[other, slot] = base_ref[asked_s[other, 0, slot]]
+            send[other, slot] = base[asked_s[other, 0, slot]]
         give(k).start()
         return carry
 
     lax.fori_loop(1, shards, pick, 0)
     for slot in range(cap):
-        recv[db, slot] = base_ref[asked_s[db, 0, slot]]
-
-    wall_own(0)
+        recv[db, slot] = base[asked_s[db, 0, slot]]
 
     heads_local = query_ref.shape[1] // head
     tokens = query_ref.shape[0]
@@ -228,12 +234,21 @@
         return carry
 
     lax.fori_loop(0, heads_local, prepare, 0)
+    kv_copy.wait()
+
+    def split(t, carry):
+        span = pl.ds(pl.multiple_of(t * 32, 32), 32)
+        kv[:, span, :] = jnp.transpose(kv_raw[span], (1, 0, 2))
+        return carry
+
+    lax.fori_loop(0, features // 32, split, 0)
+    for h in range(group):
+        value_s[:, pl.ds(h * pair + head, head)] = jnp.ones((per * positions, head), jnp.bfloat16)
 
     wall_near(0)
     wall_own(1)
     wall_far(0)
     wall_near(1)
-    wall_far(1)
 
     def give_wait(k, carry):
         give(k).wait()
@@ -254,6 +269,7 @@
         return carry
 
     lax.fori_loop(1, group, choose, 0)
+    wall_far(1)
     for slot in range(per):
         place = target_ref[me * per + slot]
         parts[me, slot] = recv[place // cap, lax.rem(place, cap)]
@@ -274,7 +290,6 @@
         lax.broadcasted_iota(jnp.int32, (pair, pair), 1) // head
     )
     average = jnp.where(same, 1.0 / head, 0.0).astype(jnp.bfloat16)
-    ones = jnp.ones((positions, head), jnp.bfloat16)
 
     def unit_pair(tensor):
         square = (tensor * tensor).astype(jnp.bfloat16)
@@ -290,9 +305,12 @@
             left, right, (((1,), (1,)), ((), ())), preferred_element_type=jnp.float32
         )
 
+    def put_values(p, value):
+        value_s[:, pl.ds(2 * p * pair, head)] = value[:, :head]
+        value_s[:, pl.ds((2 * p + 1) * pair, head)] = value[:, head:]
+
     out_copy.wait()
     for layer in range(layers):
-        own_copies[layer].wait()
         for chunk in (at_twin, up_twin, down_twin, far_twin):
             for piece in range(2):
                 wall_arrived(layer, chunk, piece)
@@ -302,21 +320,18 @@
         for p in range(group // 2):
             lanes = pl.ds(p * pair, pair)
             query = unit_pair(product(normed[...], wall[layer, 0, :, lanes])) * scale
-            key = unit_pair(product(normed[...], wall[layer, 1, :, lanes])).astype(jnp.bfloat16)
+            query_s[:, lanes] = query.astype(jnp.bfloat16)
+            key = unit_pair(product(normed[...], wall[layer, 1, :, lanes]))
+            key_s[:, lanes] = key.astype(jnp.bfloat16)
             value = product(normed[...], wall[layer, 2, :, lanes]).astype(jnp.bfloat16)
-            query = query.astype(jnp.bfloat16)
-            for h in range(2):
-                here = slice(h * head, (h + 1) * head)
-                for slot in range(per):
-                    span = slice(slot * positions, (slot + 1) * positions)
-                    weights = jnp.exp2(against(query[span, here], key[span, here]))
-                    mixed = product(
-                        weights.astype(jnp.bfloat16),
-                        jnp.concatenate([value[span, here], ones], axis=1),
-                    )
-                    attended[
-                        pl.ds(slot * positions, positions), pl.ds(p * pair + h * head, head)
-                    ] = (mixed[:, :head] / mixed[:, head:]).astype(jnp.bfloat16)
+            put_values(p, value)
+        for h in range(group):
+            lanes = pl.ds(h * head, head)
+            for slot in range(per):
+                span = pl.ds(slot * positions, positions)
+                weights = jnp.exp2(against(query_s[span, lanes], key_s[span, lanes]))
+                mixed = product(weights.astype(jnp.bfloat16), value_s[span, pl.ds(h * pair, pair)])
+                attended[span, lanes] = (mixed[:, :head] / mixed[:, head:]).astype(jnp.bfloat16)
         for t in range(features // 256):
             lanes = pl.ds(t * 256, 256)
             hidden[:, lanes] += product(attended[...], wout[layer, :, lanes])
@@ -341,7 +356,6 @@
         ship(2 + piece, me, 1 - piece, to_down)
     for piece in range(2):
         ship(4 + piece, me, piece, to_twin)
-    kv_copy.wait()
 
     def cross(step, carry):
         @pl.when(step == 1)
@@ -395,25 +409,17 @@
         span = pl.ds(pl.multiple_of(chunk * BL, BL), BL)
         for p in range(heads_local // 2):
             lanes = pl.ds(p * pair, pair)
-            key = unit_pair(product(chunks[chunk], kv[0, :, lanes])).astype(jnp.bfloat16)
-            value = product(chunks[chunk], kv[1, :, lanes]).astype(jnp.bfloat16)
-            for h in range(2):
-                here = slice(h * head, (h + 1) * head)
-                weights = jnp.exp2(
-                    against(queries[span, pl.ds(p * pair + h * head, head)], key[:, here])
-                )
-                weights = jnp.concatenate(
-                    [weights[:, :positions], weights[:, positions:] * alive], axis=1
-                ).astype(jnp.bfloat16)
-                mixed = product(
-                    weights,
-                    jnp.concatenate(
-                        [value[:, here], jnp.concatenate([ones, ones], axis=0)], axis=1
-                    ),
-                )
-                mix_ref[span, pl.ds(p * pair + h * head, head)] = (
-                    mixed[:, :head] / mixed[:, head:]
-                ).astype(jnp.bfloat16)
+            key = unit_pair(product(chunks[chunk], kv[0, :, lanes]))
+            key_s[:, lanes] = key.astype(jnp.bfloat16)
+            put_values(p, product(chunks[chunk], kv[1, :, lanes]).astype(jnp.bfloat16))
+        for h in range(heads_local):
+            lanes = pl.ds(h * head, head)
+            weights = jnp.exp2(against(queries[span, lanes], key_s[:, lanes]))
+            weights = jnp.concatenate(
+                [weights[:, :positions], weights[:, positions:] * alive], axis=1
+            )
+            mixed = product(weights.astype(jnp.bfloat16), value_s[:, pl.ds(h * pair, pair)])
+            mix_ref[span, lanes] = (mixed[:, :head] / mixed[:, head:]).astype(jnp.bfloat16)
         return carry
 
     lax.fori_loop(0, blocks, cross, 0)
@@ -424,8 +430,8 @@
         copy.wait_send()
 
 
-def retrieve(shards, group, cap, ask, target, base, live, gain, final, query, own, out, kv):
-    _, positions, head = base.shape
+def retrieve(shards, group, cap, ask, target, data, live, gain, final, query, own, out, kv):
+    positions, per_shard, head = data.shape
     layers, features = gain.shape
     per = target.shape[0] // group
     tokens = query.shape[0]
@@ -437,20 +443,27 @@
         in_specs=[VMEM, SMEM, VMEM, SMEM, VMEM, VMEM, VMEM, ANY, ANY, ANY],
         out_specs=VMEM,
         scratch_shapes=[
+            pltpu.VMEM((per_shard, positions, head), bf16),
             pltpu.VMEM((shards, 1, 128), jnp.int32),
             pltpu.SMEM((shards, 1, 128), jnp.int32),
             pltpu.VMEM((shards, cap, positions, head), bf16),
             pltpu.VMEM((shards, cap, positions, head), bf16),
             pltpu.VMEM((group, per, positions, head), bf16),
             pltpu.VMEM((group, per, positions, head), bf16),
+            pltpu.VMEM(own.shape, bf16),
+            pltpu.VMEM((layers, 3, features, head), bf16),
             pltpu.VMEM((layers, 3, features, features), bf16),
             pltpu.VMEM(out.shape, bf16),
             pltpu.VMEM(kv.shape, bf16),
+            pltpu.VMEM((2, features, kv.shape[2]), bf16),
             pltpu.VMEM((per * positions, features), f32),
             pltpu.VMEM((per * positions, features), bf16),
             pltpu.VMEM((per * positions, features), bf16),
             pltpu.VMEM((tokens + BL, head), f32),
             pltpu.VMEM(query.shape, bf16),
+            pltpu.VMEM((per * positions, group * head), bf16),
+            pltpu.VMEM((per * positions, group * head), bf16),
+            pltpu.VMEM((per * positions, group * 2 * head), bf16),
             pltpu.VMEM((group, per * positions, features), bf16),
             dma((shards,)),
             dma((shards,)),
@@ -459,7 +472,7 @@
             dma((group,)),
             dma((group,)),
             dma,
-            dma((layers,)),
+            dma,
             dma,
             dma,
             dma((layers, 14)),
@@ -470,7 +483,7 @@
         compiler_params=pltpu.CompilerParams(
             collective_id=0, has_side_effects=True, vmem_limit_bytes=52 * 2**20
         ),
-    )(ask, target, base, live, gain, final, query, own, out, kv)
+    )(ask, target, data, live, gain, final, query, own, out, kv)
 
 
 def on_device(
@@ -502,21 +515,20 @@
     inside = jnp.arange(128)[None, :, None] < capacity
     matched = ((target[None, None, :] == buckets[:, :, None]) & inside).astype(jnp.int32)
     outgoing = jnp.sum(matched * within[None, None, :], axis=2).reshape(shards, 1, 128)
-    by_row = database.transpose(1, 0, 2)
     mixed = retrieve(
         shards,
         group,
         capacity,
         outgoing,
         target,
-        by_row,
+        database,
         live_counts,
         enc_gain,
         final_gain.reshape(1, -1),
         queries,
-        enc_qkv.transpose(0, 2, 1, 3),
+        enc_qkv,
         enc_out,
-        kv_weight.transpose(1, 0, 2),
+        kv_weight,
     )
     tokens, width = queries.shape
     front = jnp.zeros((BL - 1, width), mixed.dtype)

time: 143 us -> 121 us (0.85)
  Pallas kernels: 132 us -> 113 us
  local copies, waits for them, and re-layouts: 10.9 us -> 6.97 us
    pallas_call x1, Pallas kernels: 132 us -> 113 us  [retrieve(): pl.pallas_call(functools.partial(kernel, shards, group, cap, 3.0 / math.s...]
    unnamed x11 -> x10, local copies, waits for them, and re-layouts: 8.85 us -> 4.9 us
where the time goes in v4:
time: 121 us; the launch traced here: 120 us
  Pallas kernels  113 us (93%)
  local copies, waits for them, and re-layouts  6.97 us (6%)
    pallas_call x1, Pallas kernels, retrieve(): pl.pallas_call(functools.partial(kernel, shards, group, cap, 3.0 / math.s...  113 us
    unnamed x10, local copies, waits for them, and re-layouts  4.9 us

profile of v4, /device:TPU:1, one launch (start us, length us, event | category | flops | bytes accessed | tf_op | source)
XLA Modules:
  0.0 120.3 jit_solution(10004867612317337815)
XLA Ops:
  0.0 0.0 copy-start
  0.0 0.0 copy-start.2
  0.0 0.0 copy-start.1
  0.0 0.0 copy-start.3
  0.0 0.8 copy.17
  0.8 0.1 reshape.196
  0.9 0.1 reshape.195
  1.0 0.0 copy-done
  1.0 0.6 gather_fusion
  1.7 0.2 convert_reduce_fusion
  1.9 0.1 iota_add_fusion
  1.9 0.2 select_reduce_fusion
  2.1 4.1 %copy.19.own_hbm = bf16[2,1024,3,128]{3,2,1,0:T(4,128)(2,1)} copy(bf16[2,1024,3,128]{3,1,2,0:T(8,128)(2,1)} %param.16) | data formatting | bytes 3145728 | tf_op args[6]
  6.2 0.0 copy-done.2
  6.2 0.0 copy-done.1
  6.2 0.0 copy-done.3
  6.2 112.8 %shard_map.100 = bf16[512,1024]{1,0:T(8,128)(2,1)S(1)} custom-call(s32[32,1,128]{2,1,0:T(1,128)S(1)} %bitcast.4, s32[16]{0:T(128)S(1)} %get-tuple-element.8.target_ref, bf16[128,32,128]{2,1,0:T(8,128)(2,1)} %data_ref.1, s32[8]{0:T(128)S(1)} %copy-done.3, f32[2,1024]{1,0:T(2,128)S(1)} %copy-done.1, f32[1,1024]{1,0:T(1,128)S(1)} %bitcast.5, ...), custom_call_target="tpu_custom_call" | custom-call | tf_op jit(solution)/shard_map/pallas_call | solution.py:440
  119.1 0.1 slice.3
  119.1 1.2 %concatenate.3 = bf16[512,1024]{1,0:T(8,128)(2,1)} pad(bf16[449,1024]{1,0:T(8,128)(2,1)S(1)} %slice.3, bf16[]{:T(256)} %constant.50.clone.1), padding=63_0x0_0 | pad | bytes 1968130 | tf_op jit(solution)/shard_map/concatenate | solution.py:535
  (6 shorter events, 0.0 us)
Async XLA Ops:
  0.0 1.0 copy-start
  0.0 6.2 %copy-start.2 = (f32[1024]{0:T(1024)S(1)}, f32[1024]{0:T(1024)}, u32[]{:S(2)}) copy-start(f32[1024]{0:T(1024)} %param.18) | copy-start | bytes 12292
  0.0 6.2 %copy-start.1 = (f32[2,1024]{1,0:T(2,128)S(1)}, f32[2,1024]{1,0:T(2,128)}, u32[]{:S(2)}) copy-start(f32[2,1024]{1,0:T(2,128)} %gain_ref.1) | copy-start | bytes 24580
  0.0 6.2 %copy-start.3 = (s32[8]{0:T(128)S(1)}, s32[8]{0:T(128)}, u32[]{:S(2)}) copy-start(s32[8]{0:T(128)} %live_ref.1) | copy-start | bytes 100

commit v5 on v4

v5 whole, which is shorter than its diff:
```python
import functools
import math

import jax
import jax.numpy as jnp
from jax import lax
from jax.experimental import pallas as pl
from jax.experimental.pallas import tpu as pltpu
from jax.sharding import PartitionSpec as P

BL = 64
GROUP = ("mp", "section")
MESH = pl.DeviceIdType.MESH
VMEM = pl.BlockSpec(memory_space=pltpu.VMEM)
SMEM = pl.BlockSpec(memory_space=pltpu.SMEM)
ANY = pl.BlockSpec(memory_space=pl.ANY)


def unit(tensor):
    return tensor * lax.rsqrt(jnp.mean(tensor * tensor, axis=-1, keepdims=True) + 1e-06)


def remote(src, dst, send_sem, recv_sem, device):
    return pltpu.make_async_remote_copy(
        src_ref=src,
        dst_ref=dst,
        send_sem=send_sem,
        recv_sem=recv_sem,
        device_id=device,
        device_id_type=MESH,
    )


def kernel(
    shards,
    group,
    cap,
    scale,
    ask_ref,
    plan_ref,
    data_ref,
    live_ref,
    gain_ref,
    final_ref,
    query_ref,
    own_hbm,
    out_hbm,
    kv_hbm,
    mix_ref,
    base,
    asked,
    asked_s,
    send,
    early,
    late,
    rows,
    parts,
    own,
    wall,
    wout,
    kv_raw,
    kv,
    hidden,
    normed,
    attended,
    stage,
    queries,
    query_s,
    key_s,
    value_s,
    chunks,
    sums,
    ask_send,
    ask_recv,
    row_send,
    row_recv,
    part_send,
    part_recv,
    asked_sem,
    own_sem,
    out_sem,
    kv_sem,
    wall_send,
    wall_recv,
    chunk_send,
    chunk_recv,
):
    sections = 2
    chips = group // sections
    db = lax.axis_index("db")
    y = lax.axis_index("mp")
    c = lax.axis_index("section")
    me = y * sections + c
    up, down, far = lax.rem(y + 1, chips), lax.rem(y + chips - 1, chips), lax.rem(y + 2, chips)
    to_up, to_down, to_twin = {"mp": up}, {"mp": down}, {"section": 1 - c}
    at_up, at_down, at_far = up * sections + c, down * sections + c, far * sections + c
    at_twin = y * sections + 1 - c
    up_twin, down_twin, far_twin = (place * sections + 1 - c for place in (up, down, far))

    layers, features = gain_ref.shape
    positions, head = base.shape[1], base.shape[2]
    batches = rows.shape[0]
    first = cap // batches
    pair = 2 * head
    blocks = live_ref.shape[0]

    own_copy = pltpu.make_async_copy(own_hbm, own, own_sem)
    out_copy = pltpu.make_async_copy(out_hbm, wout, out_sem)
    kv_copy = pltpu.make_async_copy(kv_hbm, kv_raw, kv_sem)
    for copy in (own_copy, out_copy, kv_copy):
        copy.start()

    def db_at(k):
        return {"db": lax.rem(db + k, shards)}

    def group_at(k):
        other = lax.rem(me + k, group)
        return other, {"mp": other // sections, "section": lax.rem(other, sections)}

    barrier = pltpu.get_barrier_semaphore()

    def greet_db(k, carry):
        pl.semaphore_signal(barrier, inc=1, device_id=db_at(k), device_id_type=MESH)
        return carry

    def greet_group(k, carry):
        pl.semaphore_signal(barrier, inc=1, device_id=group_at(k)[1], device_id_type=MESH)
        return carry

    lax.fori_loop(1, shards, greet_db, 0)
    lax.fori_loop(1, group, greet_group, 0)
    mine = pl.ds(pl.multiple_of(me * head, head), head)
    own_copy.wait()
    for layer in range(layers):
        wall[layer, :, :, mine] = own[layer]
    base[...] = jnp.transpose(data_ref[...], (1, 0, 2))
    pl.semaphore_wait(barrier, shards + group - 2)

    def ask(k):
        other = lax.rem(db + k, shards)
        return remote(ask_ref.at[other], asked.at[db], ask_send.at[k], ask_recv.at[k], db_at(k))

    def ask_start(k, carry):
        ask(k).start()
        return carry

    lax.fori_loop(1, shards, ask_start, 0)
    asked[pl.ds(db, 1)] = ask_ref[pl.ds(db, 1)]

    half_rows = features // 2

    def wall_place(layer, chunk, piece):
        return wall.at[
            layer,
            :,
            pl.ds(piece * half_rows, half_rows),
            pl.ds(pl.multiple_of(chunk * head, head), head),
        ]

    def wall_ship(number, layer, chunk, piece, device, local=False):
        place = wall_place(layer, chunk, piece)
        source = own.at[layer, :, pl.ds(piece * half_rows, half_rows), :] if local else place
        copy = remote(
            source, place, wall_send.at[layer, number], wall_recv.at[layer, chunk, piece], device
        )
        copy.start()
        return copy

    def wall_arrived(layer, chunk, piece):
        place = wall_place(layer, chunk, piece)
        remote(
            place, place, wall_send.at[layer, 0], wall_recv.at[layer, chunk, piece], to_twin
        ).wait_recv()

    sent = []

    def wall_own(layer):
        for piece in range(2):
            sent.append(wall_ship(piece, layer, me, piece, to_up, True))
            sent.append(wall_ship(2 + piece, layer, me, 1 - piece, to_down, True))
        for piece in range(2):
            sent.append(wall_ship(4 + piece, layer, me, piece, to_twin, True))

    def wall_near(layer):
        wall_arrived(layer, at_down, 0)
        sent.append(wall_ship(6, layer, at_down, 0, to_up))
        sent.append(wall_ship(7, layer, at_down, 0, to_twin))
        wall_arrived(layer, at_up, 1)
        sent.append(wall_ship(8, layer, at_up, 1, to_down))
        sent.append(wall_ship(9, layer, at_up, 1, to_twin))
        wall_arrived(layer, at_down, 1)
        sent.append(wall_ship(10, layer, at_down, 1, to_twin))
        wall_arrived(layer, at_up, 0)
        sent.append(wall_ship(11, layer, at_up, 0, to_twin))

    def wall_far(layer):
        for piece in range(2):
            wall_arrived(layer, at_far, piece)
            sent.append(wall_ship(12 + piece, layer, at_far, piece, to_twin))

    wall_own(0)

    def ask_wait(k, carry):
        ask(k).wait()
        return carry

    lax.fori_loop(1, shards, ask_wait, 0)
    to_scalar = pltpu.make_async_copy(asked, asked_s, asked_sem)
    to_scalar.start()
    to_scalar.wait()

    def give(k, batch):
        other = lax.rem(db + k, shards)
        return remote(
            send.at[other, pl.ds(batch * first, first)],
            (early, late)[batch].at[db],
            row_send.at[batch, k],
            row_recv.at[batch, k],
            db_at(k),
        )

    for batch in range(batches):

        def pick(k, carry, batch=batch):
            other = lax.rem(db + k, shards)
            for slot in range(batch * first, (batch + 1) * first):
                send[other, slot] = base[asked_s[other, 0, slot]]
            give(k, batch).start()
            return carry

        lax.fori_loop(1, shards, pick, 0)
    for slot in range(first):
        early[db, slot] = base[asked_s[db, 0, slot]]
        late[db, slot] = base[asked_s[db, 0, first + slot]]

    heads_local = query_ref.shape[1] // head
    tokens = query_ref.shape[0]

    def prepare(h, carry):
        lanes = pl.ds(pl.multiple_of(h * head, head), head)
        stage[pl.ds(0, tokens)] = unit(query_ref[:, lanes].astype(jnp.float32)) * scale
        stage[pl.ds(tokens, BL)] = jnp.zeros((BL, head), jnp.float32)
        shifted = stage[pl.ds(BL - 1, tokens)].astype(jnp.bfloat16)
        queries[:, :, lanes] = shifted.reshape(blocks, BL, head)
        return carry

    lax.fori_loop(0, heads_local, prepare, 0)
    kv_copy.wait()

    def split(t, carry):
        span = pl.ds(pl.multiple_of(t * 32, 32), 32)
        kv[:, span, :] = jnp.transpose(kv_raw[span], (1, 0, 2))
        return carry

    lax.fori_loop(0, features // 32, split, 0)
    for h in range(group):
        value_s[:, pl.ds(h * pair + head, head)] = jnp.ones((value_s.shape[0], head), jnp.bfloat16)

    wall_near(0)
    wall_own(1)
    wall_far(0)

    def give_wait(batch):
        def one(k, carry):
            give(k, batch).wait()
            return carry

        lax.fori_loop(1, shards, one, 0)

    def part(k, batch):
        other, device = group_at(k)
        return remote(
            rows.at[batch, other],
            parts.at[batch, me],
            part_send.at[batch, k],
            part_recv.at[batch, k],
            device,
        )

    def chosen(batch, number):
        place = plan_ref[batch * group + number]
        holder, slot = place // cap, lax.rem(place, cap)
        row = early[holder, jnp.minimum(slot, first - 1)]
        if batch == 0:
            return row
        return jnp.where(slot < first, row, late[holder, jnp.maximum(slot - first, 0)])

    def part_start(batch):
        def one(k, carry):
            other = lax.rem(me + k, group)
            rows[batch, other] = chosen(batch, other)
            part(k, batch).start()
            return carry

        lax.fori_loop(1, group, one, 0)
        parts[batch, me] = chosen(batch, me)

    def part_wait(batch):
        def one(k, carry):
            part(k, batch).wait()
            return carry

        lax.fori_loop(1, group, one, 0)
        for source in range(group):
            hidden[batch, :, pl.ds(source * head, head)] = parts[batch, source].astype(jnp.float32)

    same = lax.broadcasted_iota(jnp.int32, (pair, pair), 0) // head == (
        lax.broadcasted_iota(jnp.int32, (pair, pair), 1) // head
    )
    average = jnp.where(same, 1.0 / head, 0.0).astype(jnp.bfloat16)

    def unit_pair(tensor):
        square = (tensor * tensor).astype(jnp.bfloat16)
        return tensor * lax.rsqrt(
            jnp.dot(square, average, preferred_element_type=jnp.float32) + 1e-06
        )

    def product(left, right):
        return jnp.dot(left, right, preferred_element_type=jnp.float32)

    def against(left, right):
        return lax.dot_general(
            left, right, (((1,), (1,)), ((), ())), preferred_element_type=jnp.float32
        )

    def put_values(p, value):
        rows_of = pl.ds(0, value.shape[0])
        value_s[rows_of, pl.ds(2 * p * pair, head)] = value[:, :head]
        value_s[rows_of, pl.ds((2 * p + 1) * pair, head)] = value[:, head:]

    def wall_wait(layer):
        for chunk in (at_twin, up_twin, down_twin, far_twin):
            for piece in range(2):
                wall_arrived(layer, chunk, piece)

    span = pl.ds(0, positions)

    def encode(batch, layer):
        normed[...] = (unit(hidden[batch]) * gain_ref[pl.ds(layer, 1)]).astype(jnp.bfloat16)
        for p in range(group // 2):
            lanes = pl.ds(p * pair, pair)
            query = unit_pair(product(normed[...], wall[layer, 0, :, lanes])) * scale
            query_s[:, lanes] = query.astype(jnp.bfloat16)
            key = unit_pair(product(normed[...], wall[layer, 1, :, lanes]))
            key_s[span, lanes] = key.astype(jnp.bfloat16)
            put_values(p, product(normed[...], wall[layer, 2, :, lanes]).astype(jnp.bfloat16))
        for h in range(group):
            lanes = pl.ds(h * head, head)
            weights = jnp.exp2(against(query_s[:, lanes], key_s[span, lanes]))
            mixed = product(weights.astype(jnp.bfloat16), value_s[span, pl.ds(h * pair, pair)])
            attended[:, lanes] = (mixed[:, :head] / mixed[:, head:]).astype(jnp.bfloat16)
        for t in range(features // 256):
            lanes = pl.ds(t * 256, 256)
            hidden[batch, :, lanes] += product(attended[...], wout[layer, :, lanes])

    half = positions // 2

    def chunk_place(batch, chunk, piece):
        return chunks.at[
            batch, chunk // sections, pl.ds(lax.rem(chunk, sections) * positions + piece * half, half)
        ]

    def ship(number, batch, chunk, piece, device):
        place = chunk_place(batch, chunk, piece)
        remote(
            place, place, chunk_send.at[batch, number], chunk_recv.at[batch, chunk, piece], device
        ).start()

    def arrived(batch, chunk, piece):
        place = chunk_place(batch, chunk, piece)
        remote(
            place, place, chunk_send.at[batch, 0], chunk_recv.at[batch, chunk, piece], to_twin
        ).wait_recv()

    def finish(batch):
        encoded = (unit(hidden[batch]) * final_ref[...]).astype(jnp.bfloat16)
        chunks[batch, y, pl.ds(pl.multiple_of(c * positions, positions), positions)] = encoded
        for piece in range(2):
            ship(piece, batch, me, piece, to_up)
            ship(2 + piece, batch, me, 1 - piece, to_down)
        for piece in range(2):
            ship(4 + piece, batch, me, piece, to_twin)

    def relay_near(batch):
        arrived(batch, at_down, 0)
        ship(6, batch, at_down, 0, to_up)
        ship(7, batch, at_down, 0, to_twin)
        arrived(batch, at_up, 1)
        ship(8, batch, at_up, 1, to_down)
        ship(9, batch, at_up, 1, to_twin)
        arrived(batch, at_down, 1)
        ship(10, batch, at_down, 1, to_twin)
        arrived(batch, at_up, 0)
        ship(11, batch, at_up, 0, to_twin)

    def relay_far(batch):
        for piece in range(2):
            arrived(batch, at_far, piece)
            ship(12 + piece, batch, at_far, piece, to_twin)

    def twin_wait(batch, chunk):
        for piece in range(2):
            arrived(batch, chunk, piece)

    def cross(batch, chip):
        tokens_here = chunks.at[batch, chip]
        for p in range(heads_local // 2):
            lanes = pl.ds(p * pair, pair)
            key = unit_pair(product(tokens_here[...], kv[0, :, lanes]))
            key_s[:, lanes] = key.astype(jnp.bfloat16)
            put_values(p, product(tokens_here[...], kv[1, :, lanes]).astype(jnp.bfloat16))
        for core in range(sections):
            place = batch * group + chip * sections + core
            block = plan_ref[batches * group + place]
            here = pl.ds(core * positions, positions)
            for h in range(heads_local):
                lanes = pl.ds(h * head, head)
                weights = jnp.exp2(against(queries[block, :, lanes], key_s[here, lanes]))
                sums[place, :, pl.ds(h * pair, pair)] = product(
                    weights.astype(jnp.bfloat16), value_s[here, pl.ds(h * pair, pair)]
                )

    give_wait(0)
    part_start(0)
    out_copy.wait()
    wall_wait(0)
    part_wait(0)
    encode(0, 0)
    wall_near(1)
    wall_far(1)
    give_wait(1)
    part_start(1)
    wall_wait(1)
    encode(0, 1)
    finish(0)
    part_wait(1)
    encode(1, 0)
    relay_near(0)
    encode(1, 1)
    finish(1)
    relay_far(0)

    def step(number, carry):
        batch = number // chips
        turn = lax.rem(number, chips)

        @pl.when(number == 0)
        def _():
            twin_wait(0, at_twin)

        @pl.when(number == 1)
        def _():
            twin_wait(0, down_twin)

        @pl.when(number == 2)
        def _():
            twin_wait(0, up_twin)
            relay_near(1)

        @pl.when(number == 3)
        def _():
            twin_wait(0, far_twin)

        @pl.when(number == 4)
        def _():
            twin_wait(1, at_twin)
            relay_far(1)

        @pl.when(number == 5)
        def _():
            twin_wait(1, down_twin)

        @pl.when(number == 6)
        def _():
            twin_wait(1, up_twin)

        @pl.when(number == 7)
        def _():
            twin_wait(1, far_twin)

        chip = jnp.where(
            turn == 0, y, jnp.where(turn == 1, down, jnp.where(turn == 2, up, far))
        )
        cross(batch, chip)
        return carry

    lax.fori_loop(0, batches * chips, step, 0)

    def combine(block, carry):
        at = 2 * batches * group + 2 * block
        one, two = plan_ref[at], plan_ref[at + 1]
        alive = (live_ref[block] > 1).astype(jnp.float32)
        span = pl.ds(pl.multiple_of(block * BL, BL), BL)
        for h in range(heads_local):
            lanes = pl.ds(h * pair, pair)
            mixed = sums[one, :, lanes] + sums[two, :, lanes] * alive
            mix_ref[span, pl.ds(h * head, head)] = (mixed[:, :head] / mixed[:, head:]).astype(
                jnp.bfloat16
            )
        return carry

    lax.fori_loop(0, blocks, combine, 0)
    for batch in range(batches):
        for number in range(14):
            place = chunk_place(batch, me, 0)
            remote(
                place, place, chunk_send.at[batch, number], chunk_recv.at[batch, me, 0], to_twin
            ).wait_send()
    for copy in sent:
        copy.wait_send()


def retrieve(shards, group, cap, ask, plan, data, live, gain, final, query, own, out, kv):
    positions, per_shard, head = data.shape
    layers, features = gain.shape
    batches = 2
    blocks = live.shape[0]
    tokens = query.shape[0]
    chips = group // 2
    dma = pltpu.SemaphoreType.DMA
    bf16, f32 = jnp.bfloat16, jnp.float32
    return pl.pallas_call(
        functools.partial(kernel, shards, group, cap, 3.0 / math.sqrt(head) * math.log2(math.e)),
        out_shape=jax.ShapeDtypeStruct(query.shape, bf16),
        in_specs=[VMEM, SMEM, VMEM, SMEM, VMEM, VMEM, VMEM, ANY, ANY, ANY],
        out_specs=VMEM,
        scratch_shapes=[
            pltpu.VMEM((per_shard, positions, head), bf16),
            pltpu.VMEM((shards, 1, 128), jnp.int32),
            pltpu.SMEM((shards, 1, 128), jnp.int32),
            pltpu.VMEM((shards, cap, positions, head), bf16),
            pltpu.VMEM((shards, cap // 2, positions, head), bf16),
            pltpu.VMEM((shards, cap // 2, positions, head), bf16),
            pltpu.VMEM((batches, group, positions, head), bf16),
            pltpu.VMEM((batches, group, positions, head), bf16),
            pltpu.VMEM(own.shape, bf16),
            pltpu.VMEM((layers, 3, features, features), bf16),
            pltpu.VMEM(out.shape, bf16),
            pltpu.VMEM(kv.shape, bf16),
            pltpu.VMEM((2, features, kv.shape[2]), bf16),
            pltpu.VMEM((batches, positions, features), f32),
            pltpu.VMEM((positions, features), bf16),
            pltpu.VMEM((positions, features), bf16),
            pltpu.VMEM((tokens + BL, head), f32),
            pltpu.VMEM((blocks, BL, query.shape[1]), bf16),
            pltpu.VMEM((positions, group * head), bf16),
            pltpu.VMEM((2 * positions, group * head), bf16),
            pltpu.VMEM((2 * positions, group * 2 * head), bf16),
            pltpu.VMEM((batches, chips, 2 * positions, features), bf16),
            pltpu.VMEM((batches * group, BL, 2 * query.shape[1]), f32),
            dma((shards,)),
            dma((shards,)),
            dma((batches, shards)),
            dma((batches, shards)),
            dma((batches, group)),
            dma((batches, group)),
            dma,
            dma,
            dma,
            dma,
            dma((layers, 14)),
            dma((layers, group, 2)),
            dma((batches, 14)),
            dma((batches, group, 2)),
        ],
        compiler_params=pltpu.CompilerParams(
            collective_id=0, has_side_effects=True, vmem_limit_bytes=60 * 2**20
        ),
    )(ask, plan, data, live, gain, final, query, own, out, kv)


def on_device(
    queries,
    database,
    neighbour_ids,
    live_counts,
    entry_rows,
    enc_gain,
    enc_qkv,
    enc_out,
    final_gain,
    kv_weight,
):
    shards = lax.axis_size("db")
    group = lax.axis_size(GROUP)
    per_shard = database.shape[1]
    wanted = neighbour_ids.reshape(-1)
    requests = wanted.shape[0]
    capacity = max(2, (requests + shards - 1) // shards)
    located = jnp.take(entry_rows, wanted)
    holder = located // per_shard
    within = located % per_shard
    ordinal = jnp.arange(requests)
    before = (holder[:, None] == holder[None, :]) & (ordinal[None, :] < ordinal[:, None])
    standing = jnp.sum(before.astype(jnp.int32), axis=1)
    target = holder * capacity + standing
    early = standing < capacity // 2
    earlier = jnp.sum((early[None, :] & (ordinal[None, :] < ordinal[:, None])).astype(jnp.int32), axis=1)
    batch_size = requests // 2
    place = jnp.where(
        early & (earlier < batch_size),
        earlier,
        batch_size + ordinal - jnp.minimum(earlier, batch_size),
    )
    seated = (place[None, :] == ordinal[:, None]).astype(jnp.int32)
    block_of = ordinal // neighbour_ids.shape[1]
    plan = jnp.concatenate(
        [jnp.sum(seated * target[None, :], axis=1), jnp.sum(seated * block_of[None, :], axis=1), place]
    )
    buckets = jnp.arange(shards)[:, None] * capacity + jnp.arange(128)[None, :]
    inside = jnp.arange(128)[None, :, None] < capacity
    matched = ((target[None, None, :] == buckets[:, :, None]) & inside).astype(jnp.int32)
    outgoing = jnp.sum(matched * within[None, None, :], axis=2).reshape(shards, 1, 128)
    mixed = retrieve(
        shards,
        group,
        capacity,
        outgoing,
        plan,
        database,
        live_counts,
        enc_gain,
        final_gain.reshape(1, -1),
        queries,
        enc_qkv.transpose(0, 2, 1, 3),
        enc_out,
        kv_weight,
    )
    tokens, width = queries.shape
    front = jnp.zeros((BL - 1, width), mixed.dtype)
    return jnp.concatenate([front, mixed[: tokens - BL + 1]], axis=0)


def solution(mesh):
    return jax.shard_map(
        on_device,
        mesh=mesh,
        in_specs=(
            P("db", GROUP),
            P(None, "db", GROUP),
            P("db", None),
            P("db"),
            P(),
            P(),
            P(None, None, None, GROUP),
            P(),
            P(),
            P(None, None, GROUP),
        ),
        out_specs=P("db", GROUP),
        check_vma=False,
    )
```

time: 121 us -> 134 us (1.11)
  Pallas kernels: 113 us -> 128 us
  local copies, waits for them, and re-layouts: 6.97 us -> 4.02 us
  other arithmetic: 0.46 us -> 1.98 us
    pallas_call x1, Pallas kernels: 113 us -> 128 us  [retrieve(): pl.pallas_call(functools.partial(kernel, shards, group, cap, 3.0 / math.s...]
    unnamed x10 -> x3, local copies, waits for them, and re-layouts: 4.9 us -> 0.76 us
where the time goes in v5:
time: 134 us
  Pallas kernels  128 us (96%)
  local copies, waits for them, and re-layouts  4.02 us (3%)
  other arithmetic  1.98 us (1%)
    pallas_call x1, Pallas kernels, retrieve(): pl.pallas_call(functools.partial(kernel, shards, group, cap, 3.0 / math.s...  128 us

profile of v5, /device:TPU:1, one launch (start us, length us, event | category | flops | bytes accessed | tf_op | source)
XLA Modules:
  0.0 134.1 jit_solution(16942797325768566823)
XLA Ops:
  0.0 0.0 copy-start
  0.0 0.8 copy.15
  0.8 0.1 reshape.238
  0.9 0.1 reshape.237
  1.0 0.0 copy-done
  1.0 0.6 gather_fusion
  1.6 0.2 convert_reduce_fusion.1
  1.8 0.1 convert_reduce_fusion
  2.0 0.1 select_reduce_fusion.2
  2.1 0.7 pad_add_fusion.plan_ref
  2.8 0.1 iota_add_fusion
  2.8 0.8 select_reduce_fusion
  3.6 128.0 %shard_map.100 = bf16[512,1024]{1,0:T(8,128)(2,1)} custom-call(s32[32,1,128]{2,1,0:T(1,128)} %bitcast.6, s32[48]{0:T(128)} %pad_add_fusion.plan_ref, bf16[128,32,128]{2,1,0:T(8,128)(2,1)} %data_ref.1, s32[8]{0:T(128)} %live_ref.1, f32[2,1024]{1,0:T(2,128)} %gain_ref.1, f32[1,1024]{1,0:T(1,128)} %bitcast.7, bf16[512,1024]{1,0:T(8,128)(2,1)} %query_ref.1, ...), custom_call_target="tpu_custom_call" | custom-call | tf_op jit(solution)/shard_map/pallas_call | solution.py:522
  131.6 1.2 slice.3
  132.8 1.2 concatenate.7
  (8 shorter events, 0.1 us)
Async XLA Ops:
  0.0 1.0 copy-start

commit v6 on v5

--- a/solution.py
+++ b/solution.py
@@ -52,7 +52,7 @@
     asked_s,
     send,
     early,
-    late,
+    both,
     rows,
     parts,
     own,
@@ -65,7 +65,9 @@
     attended,
     stage,
     queries,
-    query_s,
+    enc_q,
+    enc_k,
+    enc_v,
     key_s,
     value_s,
     chunks,
@@ -213,7 +215,7 @@
         other = lax.rem(db + k, shards)
         return remote(
             send.at[other, pl.ds(batch * first, first)],
-            (early, late)[batch].at[db],
+            both.at[db, pl.ds(first, first)] if batch else early.at[db],
             row_send.at[batch, k],
             row_recv.at[batch, k],
             db_at(k),
@@ -231,7 +233,7 @@
         lax.fori_loop(1, shards, pick, 0)
     for slot in range(first):
         early[db, slot] = base[asked_s[db, 0, slot]]
-        late[db, slot] = base[asked_s[db, 0, first + slot]]
+        both[db, first + slot] = base[asked_s[db, 0, first + slot]]
 
     heads_local = query_ref.shape[1] // head
     tokens = query_ref.shape[0]
@@ -253,7 +255,8 @@
         return carry
 
     lax.fori_loop(0, features // 32, split, 0)
-    for h in range(group):
+    enc_v[:, pl.ds(head, head)] = jnp.ones((enc_v.shape[0], head), jnp.bfloat16)
+    for h in range(heads_local):
         value_s[:, pl.ds(h * pair + head, head)] = jnp.ones((value_s.shape[0], head), jnp.bfloat16)
 
     wall_near(0)
@@ -280,10 +283,11 @@
     def chosen(batch, number):
         place = plan_ref[batch * group + number]
         holder, slot = place // cap, lax.rem(place, cap)
-        row = early[holder, jnp.minimum(slot, first - 1)]
-        if batch == 0:
-            return row
-        return jnp.where(slot < first, row, late[holder, jnp.maximum(slot - first, 0)])
+        return both[holder, slot] if batch else early[holder, slot]
+
+    def keep_early(k, carry):
+        both[k, pl.ds(0, first)] = early[k]
+        return carry
 
     def part_start(batch):
         def one(k, carry):
@@ -323,32 +327,37 @@
             left, right, (((1,), (1,)), ((), ())), preferred_element_type=jnp.float32
         )
 
-    def put_values(p, value):
-        rows_of = pl.ds(0, value.shape[0])
-        value_s[rows_of, pl.ds(2 * p * pair, head)] = value[:, :head]
-        value_s[rows_of, pl.ds((2 * p + 1) * pair, head)] = value[:, head:]
+    def diagonal(scores):
+        rows_in, lanes_in = scores.shape[0] // 2, scores.shape[1] // 2
+        empty = jnp.zeros((rows_in, lanes_in), jnp.float32)
+        upper = jnp.concatenate([jnp.exp2(scores[:rows_in, :lanes_in]), empty], axis=1)
+        lower = jnp.concatenate([empty, jnp.exp2(scores[rows_in:, lanes_in:])], axis=1)
+        return jnp.concatenate([upper, lower], axis=0).astype(jnp.bfloat16)
 
     def wall_wait(layer):
         for chunk in (at_twin, up_twin, down_twin, far_twin):
             for piece in range(2):
                 wall_arrived(layer, chunk, piece)
-
-    span = pl.ds(0, positions)
 
     def encode(batch, layer):
         normed[...] = (unit(hidden[batch]) * gain_ref[pl.ds(layer, 1)]).astype(jnp.bfloat16)
         for p in range(group // 2):
             lanes = pl.ds(p * pair, pair)
             query = unit_pair(product(normed[...], wall[layer, 0, :, lanes])) * scale
-            query_s[:, lanes] = query.astype(jnp.bfloat16)
             key = unit_pair(product(normed[...], wall[layer, 1, :, lanes]))
-            key_s[span, lanes] = key.astype(jnp.bfloat16)
-            put_values(p, product(normed[...], wall[layer, 2, :, lanes]).astype(jnp.bfloat16))
-        for h in range(group):
-            lanes = pl.ds(h * head, head)
-            weights = jnp.exp2(against(query_s[:, lanes], key_s[span, lanes]))
-            mixed = product(weights.astype(jnp.bfloat16), value_s[span, pl.ds(h * pair, pair)])
-            attended[:, lanes] = (mixed[:, :head] / mixed[:, head:]).astype(jnp.bfloat16)
+            value = product(normed[...], wall[layer, 2, :, lanes])
+            for h in range(2):
+                here = slice(h * head, (h + 1) * head)
+                stack = pl.ds((2 * p + h) * positions, positions)
+                enc_q[stack] = query[:, here].astype(jnp.bfloat16)
+                enc_k[stack] = key[:, here].astype(jnp.bfloat16)
+                enc_v[stack, pl.ds(0, head)] = value[:, here].astype(jnp.bfloat16)
+        for p in range(group // 2):
+            stack = pl.ds(2 * p * positions, 2 * positions)
+            mixed = product(diagonal(against(enc_q[stack], enc_k[stack])), enc_v[stack])
+            mixed = (mixed[:, :head] / mixed[:, head:]).astype(jnp.bfloat16)
+            attended[:, pl.ds(p * pair, head)] = mixed[:positions]
+            attended[:, pl.ds(p * pair + head, head)] = mixed[positions:]
         for t in range(features // 256):
             lanes = pl.ds(t * 256, 256)
             hidden[batch, :, lanes] += product(attended[...], wout[layer, :, lanes])
@@ -408,17 +417,22 @@
             lanes = pl.ds(p * pair, pair)
             key = unit_pair(product(tokens_here[...], kv[0, :, lanes]))
             key_s[:, lanes] = key.astype(jnp.bfloat16)
-            put_values(p, product(tokens_here[...], kv[1, :, lanes]).astype(jnp.bfloat16))
-        for core in range(sections):
-            place = batch * group + chip * sections + core
-            block = plan_ref[batches * group + place]
-            here = pl.ds(core * positions, positions)
-            for h in range(heads_local):
-                lanes = pl.ds(h * head, head)
-                weights = jnp.exp2(against(queries[block, :, lanes], key_s[here, lanes]))
-                sums[place, :, pl.ds(h * pair, pair)] = product(
-                    weights.astype(jnp.bfloat16), value_s[here, pl.ds(h * pair, pair)]
-                )
+            value = product(tokens_here[...], kv[1, :, lanes]).astype(jnp.bfloat16)
+            value_s[:, pl.ds(2 * p * pair, head)] = value[:, :head]
+            value_s[:, pl.ds((2 * p + 1) * pair, head)] = value[:, head:]
+        one = batch * group + chip * sections
+        first_block = plan_ref[batches * group + one]
+        second_block = plan_ref[batches * group + one + 1]
+        for h in range(heads_local):
+            lanes = pl.ds(h * head, head)
+            query = jnp.concatenate(
+                [queries[first_block, :, lanes], queries[second_block, :, lanes]], axis=0
+            )
+            mixed = product(
+                diagonal(against(query, key_s[:, lanes])), value_s[:, pl.ds(h * pair, pair)]
+            )
+            sums[one, :, pl.ds(h * pair, pair)] = mixed[:BL]
+            sums[one + 1, :, pl.ds(h * pair, pair)] = mixed[BL:]
 
     give_wait(0)
     part_start(0)
@@ -426,6 +440,7 @@
     wall_wait(0)
     part_wait(0)
     encode(0, 0)
+    lax.fori_loop(0, shards, keep_early, 0)
     wall_near(1)
     wall_far(1)
     give_wait(1)
@@ -530,7 +545,7 @@
             pltpu.SMEM((shards, 1, 128), jnp.int32),
             pltpu.VMEM((shards, cap, positions, head), bf16),
             pltpu.VMEM((shards, cap // 2, positions, head), bf16),
-            pltpu.VMEM((shards, cap // 2, positions, head), bf16),
+            pltpu.VMEM((shards, cap, positions, head), bf16),
             pltpu.VMEM((batches, group, positions, head), bf16),
             pltpu.VMEM((batches, group, positions, head), bf16),
             pltpu.VMEM(own.shape, bf16),
@@ -543,7 +558,9 @@
             pltpu.VMEM((positions, features), bf16),
             pltpu.VMEM((tokens + BL, head), f32),
             pltpu.VMEM((blocks, BL, query.shape[1]), bf16),
-            pltpu.VMEM((positions, group * head), bf16),
+            pltpu.VMEM((group * positions, head), bf16),
+            pltpu.VMEM((group * positions, head), bf16),
+            pltpu.VMEM((group * positions, 2 * head), bf16),
             pltpu.VMEM((2 * positions, group * head), bf16),
             pltpu.VMEM((2 * positions, group * 2 * head), bf16),
             pltpu.VMEM((batches, chips, 2 * positions, features), bf16),
@@ -626,9 +643,7 @@
         enc_out,
         kv_weight,
     )
-    tokens, width = queries.shape
-    front = jnp.zeros((BL - 1, width), mixed.dtype)
-    return jnp.concatenate([front, mixed[: tokens - BL + 1]], axis=0)
+    return lax.pad(mixed, jnp.zeros((), mixed.dtype), ((BL - 1, 1 - BL, 0), (0, 0, 0)))
 
 
 def solution(mesh):

time: 134 us -> 123 us (0.918)
  Pallas kernels: 128 us -> 117 us
    pallas_call x1, Pallas kernels: 128 us -> 117 us  [retrieve(): pl.pallas_call(functools.partial(kernel, shards, group, cap, 3.0 / math.s...]
    pad x0 -> x1, local copies, waits for them, and re-layouts: none -> 2.39 us  [on_device(): lax.pad(mixed, jnp.zeros((), mixed.dtype), ((BL - 1, 1 - BL, 0), (0, 0, 0)))]
where the time goes in v6:
time: 123 us
  Pallas kernels  117 us (95%)
  local copies, waits for them, and re-layouts  3.96 us (3%)
  other arithmetic  1.98 us (2%)
    pallas_call x1, Pallas kernels, retrieve(): pl.pallas_call(functools.partial(kernel, shards, group, cap, 3.0 / math.s...  117 us

profile of v6, /device:TPU:1, one launch (start us, length us, event | category | flops | bytes accessed | tf_op | source)
XLA Modules:
  0.0 123.3 jit_solution(3050936533604802542)
XLA Ops:
  0.0 0.0 copy-start
  0.0 0.8 copy.15
  0.8 0.1 reshape.238
  0.9 0.1 reshape.237
  1.0 0.0 copy-done
  1.0 0.6 gather_fusion
  1.6 0.2 convert_reduce_fusion.1
  1.8 0.1 convert_reduce_fusion
  2.0 0.1 select_reduce_fusion.2
  2.1 0.7 pad_add_fusion.plan_ref
  2.8 0.1 iota_add_fusion
  2.8 0.8 select_reduce_fusion
  3.6 117.3 %shard_map.100 = bf16[512,1024]{1,0:T(8,128)(2,1)} custom-call(s32[32,1,128]{2,1,0:T(1,128)} %bitcast.6, s32[48]{0:T(128)} %pad_add_fusion.plan_ref, bf16[128,32,128]{2,1,0:T(8,128)(2,1)} %data_ref.1, s32[8]{0:T(128)} %live_ref.1, f32[2,1024]{1,0:T(2,128)} %gain_ref.1, f32[1,1024]{1,0:T(1,128)} %bitcast.7, bf16[512,1024]{1,0:T(8,128)(2,1)} %query_ref.1, ...), custom_call_target="tpu_custom_call" | custom-call | tf_op jit(solution)/shard_map/pallas_call | solution.py:537
  120.9 2.4 %pad_slice_fusion = bf16[512,1024]{1,0:T(8,128)(2,1)} fusion(bf16[512,1024]{1,0:T(8,128)(2,1)} %shard_map.100), kind=kLoop, calls=%fused_computation.1 | loop fusion | bytes 2097152 | tf_op jit(solution)/shard_map/pad | solution.py:646
  (8 shorter events, 0.1 us)
Async XLA Ops:
  0.0 1.0 copy-start

commit v7 on v6

--- a/solution.py
+++ b/solution.py
@@ -436,12 +436,12 @@
 
     give_wait(0)
     part_start(0)
+    wall_near(1)
     out_copy.wait()
     wall_wait(0)
     part_wait(0)
     encode(0, 0)
     lax.fori_loop(0, shards, keep_early, 0)
-    wall_near(1)
     wall_far(1)
     give_wait(1)
     part_start(1)
@@ -450,49 +450,48 @@
     finish(0)
     part_wait(1)
     encode(1, 0)
-    relay_near(0)
     encode(1, 1)
     finish(1)
-    relay_far(0)
 
     def step(number, carry):
-        batch = number // chips
-        turn = lax.rem(number, chips)
-
         @pl.when(number == 0)
         def _():
             twin_wait(0, at_twin)
 
         @pl.when(number == 1)
         def _():
+            relay_near(0)
+            twin_wait(1, at_twin)
+
+        @pl.when(number == 2)
+        def _():
             twin_wait(0, down_twin)
 
-        @pl.when(number == 2)
+        @pl.when(number == 3)
         def _():
             twin_wait(0, up_twin)
+            relay_far(0)
+
+        @pl.when(number == 4)
+        def _():
             relay_near(1)
-
-        @pl.when(number == 3)
-        def _():
             twin_wait(0, far_twin)
 
-        @pl.when(number == 4)
-        def _():
-            twin_wait(1, at_twin)
+        @pl.when(number == 5)
+        def _():
+            twin_wait(1, down_twin)
+
+        @pl.when(number == 6)
+        def _():
             relay_far(1)
-
-        @pl.when(number == 5)
-        def _():
-            twin_wait(1, down_twin)
-
-        @pl.when(number == 6)
-        def _():
             twin_wait(1, up_twin)
 
         @pl.when(number == 7)
         def _():
             twin_wait(1, far_twin)
 
+        batch = jnp.where(number == 1, 1, jnp.where(number >= 5, 1, 0))
+        turn = jnp.where(number < 2, 0, jnp.where(number < 5, number - 1, number - 4))
         chip = jnp.where(
             turn == 0, y, jnp.where(turn == 1, down, jnp.where(turn == 2, up, far))
         )

time: 123 us -> 114 us (0.927)
  Pallas kernels: 117 us -> 108 us
    pallas_call x1, Pallas kernels: 117 us -> 108 us  [retrieve(): pl.pallas_call(functools.partial(kernel, shards, group, cap, 3.0 / math.s...]
where the time goes in v7:
time: 114 us
  Pallas kernels  108 us (95%)
  local copies, waits for them, and re-layouts  3.96 us (3%)
  other arithmetic  1.98 us (2%)
    pallas_call x1, Pallas kernels, retrieve(): pl.pallas_call(functools.partial(kernel, shards, group, cap, 3.0 / math.s...  108 us
    pad x1, local copies, waits for them, and re-layouts, on_device(): lax.pad(mixed, jnp.zeros((), mixed.dtype), ((BL - 1, 1 - BL, 0), (0, 0, 0)))  2.39 us

profile of v7, /device:TPU:1, one launch (start us, length us, event | category | flops | bytes accessed | tf_op | source)
XLA Modules:
  0.0 113.9 jit_solution(1470476984356112936)
XLA Ops:
  0.0 0.0 copy-start
  0.0 0.8 copy.15
  0.8 0.1 reshape.238
  0.9 0.1 reshape.237
  1.0 0.0 copy-done
  1.0 0.6 gather_fusion
  1.6 0.2 convert_reduce_fusion.1
  1.8 0.1 convert_reduce_fusion
  2.0 0.1 select_reduce_fusion.2
  2.1 0.7 pad_add_fusion.plan_ref
  2.8 0.1 iota_add_fusion
  2.8 0.8 select_reduce_fusion
  3.6 108.0 %shard_map.100 = bf16[512,1024]{1,0:T(8,128)(2,1)} custom-call(s32[32,1,128]{2,1,0:T(1,128)} %bitcast.6, s32[48]{0:T(128)} %pad_add_fusion.plan_ref, bf16[128,32,128]{2,1,0:T(8,128)(2,1)} %data_ref.1, s32[8]{0:T(128)} %live_ref.1, f32[2,1024]{1,0:T(2,128)} %gain_ref.1, f32[1,1024]{1,0:T(1,128)} %bitcast.7, bf16[512,1024]{1,0:T(8,128)(2,1)} %query_ref.1, ...), custom_call_target="tpu_custom_call" | custom-call | tf_op jit(solution)/shard_map/pallas_call | solution.py:536
  111.6 2.4 %pad_slice_fusion = bf16[512,1024]{1,0:T(8,128)(2,1)} fusion(bf16[512,1024]{1,0:T(8,128)(2,1)} %shard_map.100), kind=kLoop, calls=%fused_computation.1 | loop fusion | bytes 2097152 | tf_op jit(solution)/shard_map/pad | solution.py:645
  (8 shorter events, 0.1 us)
Async XLA Ops:
  0.0 1.0 copy-start

commit v8 on v7

--- a/solution.py
+++ b/solution.py
@@ -84,6 +84,8 @@
     kv_sem,
     wall_send,
     wall_recv,
+    side_send,
+    side_recv,
     chunk_send,
     chunk_recv,
 ):
@@ -151,17 +153,20 @@
 
     half_rows = features // 2
 
+    def ring_types(layer):
+        return pl.ds(2, 1) if layer else pl.ds(0, 3)
+
     def wall_place(layer, chunk, piece):
         return wall.at[
             layer,
-            :,
+            ring_types(layer),
             pl.ds(piece * half_rows, half_rows),
             pl.ds(pl.multiple_of(chunk * head, head), head),
         ]
 
     def wall_ship(number, layer, chunk, piece, device, local=False):
         place = wall_place(layer, chunk, piece)
-        source = own.at[layer, :, pl.ds(piece * half_rows, half_rows), :] if local else place
+        source = own.at[layer, ring_types(layer), pl.ds(piece * half_rows, half_rows), :] if local else place
         copy = remote(
             source, place, wall_send.at[layer, number], wall_recv.at[layer, chunk, piece], device
         )
@@ -200,6 +205,68 @@
             wall_arrived(layer, at_far, piece)
             sent.append(wall_ship(12 + piece, layer, at_far, piece, to_twin))
 
+    depth = max(1, shards // 4)
+    columns = shards // depth
+    x, z = db // depth, lax.rem(db, depth)
+    quarter_rows = features // columns
+
+    def side_place(chunk, quarter):
+        return wall.at[
+            1,
+            pl.ds(0, 2),
+            pl.ds(quarter * quarter_rows, quarter_rows),
+            pl.ds(pl.multiple_of(chunk * head, head), head),
+        ]
+
+    def side_ship(number, chunk, quarter, device, local=False):
+        place = side_place(chunk, quarter)
+        source = place
+        if local:
+            source = own.at[1, pl.ds(0, 2), pl.ds(quarter * quarter_rows, quarter_rows), :]
+        copy = remote(source, place, side_send.at[number], side_recv.at[chunk, quarter], device)
+        copy.start()
+        sent.append(copy)
+
+    def side_arrived(chunk, quarter):
+        place = side_place(chunk, quarter)
+        remote(place, place, side_send.at[0], side_recv.at[chunk, quarter], to_twin).wait_recv()
+
+    def side_own():
+        for k in range(1, chips):
+            side_ship(k - 1, me, x, {"mp": lax.rem(y + k, chips)}, True)
+        for quarter in range(columns):
+            side_ship(chips - 1 + quarter, me, quarter, to_twin, True)
+
+    side_base = chips - 1 + columns
+
+    def side_spread():
+        number = side_base
+        for k in range(1, chips):
+            chunk = lax.rem(y + k, chips) * sections + c
+            side_arrived(chunk, x)
+            for step in range(1, columns):
+                device = {"db": lax.rem(x + step, columns) * depth + z}
+                side_ship(number, chunk, x, device)
+                number += 1
+            side_ship(number, chunk, x, to_twin)
+            number += 1
+
+    def side_relay():
+        number = side_base + (chips - 1) * columns
+        for k in range(1, chips):
+            chunk = lax.rem(y + k, chips) * sections + c
+            for step in range(1, columns):
+                quarter = lax.rem(x + step, columns)
+                side_arrived(chunk, quarter)
+                side_ship(number, chunk, quarter, to_twin)
+                number += 1
+
+    def side_wait():
+        for k in range(chips):
+            for quarter in range(columns):
+                side_arrived(lax.rem(y + k, chips) * sections + 1 - c, quarter)
+
+    side_own()
     wall_own(0)
 
     def ask_wait(k, carry):
@@ -231,6 +298,8 @@
             return carry
 
         lax.fori_loop(1, shards, pick, 0)
+        if batch == 0:
+            side_spread()
     for slot in range(first):
         early[db, slot] = base[asked_s[db, 0, slot]]
         both[db, first + slot] = base[asked_s[db, 0, first + slot]]
@@ -434,6 +503,7 @@
             sums[one, :, pl.ds(h * pair, pair)] = mixed[:BL]
             sums[one + 1, :, pl.ds(h * pair, pair)] = mixed[BL:]
 
+    side_relay()
     give_wait(0)
     part_start(0)
     wall_near(1)
@@ -443,15 +513,10 @@
     encode(0, 0)
     lax.fori_loop(0, shards, keep_early, 0)
     wall_far(1)
-    give_wait(1)
-    part_start(1)
+    side_wait()
     wall_wait(1)
     encode(0, 1)
     finish(0)
-    part_wait(1)
-    encode(1, 0)
-    encode(1, 1)
-    finish(1)
 
     def step(number, carry):
         @pl.when(number == 0)
@@ -461,24 +526,30 @@
         @pl.when(number == 1)
         def _():
             relay_near(0)
-            twin_wait(1, at_twin)
+            twin_wait(0, down_twin)
 
         @pl.when(number == 2)
         def _():
-            twin_wait(0, down_twin)
+            give_wait(1)
+            part_start(1)
+            twin_wait(0, up_twin)
 
         @pl.when(number == 3)
         def _():
-            twin_wait(0, up_twin)
             relay_far(0)
+            part_wait(1)
+            encode(1, 0)
+            encode(1, 1)
+            finish(1)
+            twin_wait(0, far_twin)
 
         @pl.when(number == 4)
         def _():
-            relay_near(1)
-            twin_wait(0, far_twin)
+            twin_wait(1, at_twin)
 
         @pl.when(number == 5)
         def _():
+            relay_near(1)
             twin_wait(1, down_twin)
 
         @pl.when(number == 6)
@@ -490,8 +561,8 @@
         def _():
             twin_wait(1, far_twin)
 
-        batch = jnp.where(number == 1, 1, jnp.where(number >= 5, 1, 0))
-        turn = jnp.where(number < 2, 0, jnp.where(number < 5, number - 1, number - 4))
+        batch = number // chips
+        turn = lax.rem(number, chips)
         chip = jnp.where(
             turn == 0, y, jnp.where(turn == 1, down, jnp.where(turn == 2, up, far))
         )
@@ -531,6 +602,7 @@
     blocks = live.shape[0]
     tokens = query.shape[0]
     chips = group // 2
+    columns = shards // max(1, shards // 4)
     dma = pltpu.SemaphoreType.DMA
     bf16, f32 = jnp.bfloat16, jnp.float32
     return pl.pallas_call(
@@ -576,6 +648,8 @@
             dma,
             dma((layers, 14)),
             dma((layers, group, 2)),
+            dma((chips - 1 + columns + (chips - 1) * (2 * columns - 1),)),
+            dma((group, columns)),
             dma((batches, 14)),
             dma((batches, group, 2)),
         ],

time: 114 us -> 123 us (1.079)
  Pallas kernels: 108 us -> 117 us
    pallas_call x1, Pallas kernels: 108 us -> 117 us  [retrieve(): pl.pallas_call(functools.partial(kernel, shards, group, cap, 3.0 / math.s...]
where the time goes in v8:
time: 123 us
  Pallas kernels  117 us (95%)
  local copies, waits for them, and re-layouts  3.96 us (3%)
  other arithmetic  1.98 us (2%)
    pallas_call x1, Pallas kernels, retrieve(): pl.pallas_call(functools.partial(kernel, shards, group, cap, 3.0 / math.s...  117 us

profile of v8, /device:TPU:1, one launch (start us, length us, event | category | flops | bytes accessed | tf_op | source)
XLA Modules:
  0.0 123.0 jit_solution(1893053740294649610)
XLA Ops:
  0.0 0.0 copy-start
  0.0 0.8 copy.15
  0.8 0.1 reshape.238
  0.9 0.1 reshape.237
  1.0 0.0 copy-done
  1.0 0.6 gather_fusion
  1.6 0.2 convert_reduce_fusion.1
  1.8 0.1 convert_reduce_fusion
  2.0 0.1 select_reduce_fusion.2
  2.1 0.7 pad_add_fusion.plan_ref
  2.8 0.1 iota_add_fusion
  2.8 0.8 select_reduce_fusion
  3.6 117.0 %shard_map.100 = bf16[512,1024]{1,0:T(8,128)(2,1)} custom-call(s32[32,1,128]{2,1,0:T(1,128)} %bitcast.6, s32[48]{0:T(128)} %pad_add_fusion.plan_ref, bf16[128,32,128]{2,1,0:T(8,128)(2,1)} %data_ref.1, s32[8]{0:T(128)} %live_ref.1, f32[2,1024]{1,0:T(2,128)} %gain_ref.1, f32[1,1024]{1,0:T(1,128)} %bitcast.7, bf16[512,1024]{1,0:T(8,128)(2,1)} %query_ref.1, ...), custom_call_target="tpu_custom_call" | custom-call | tf_op jit(solution)/shard_map/pallas_call | solution.py:608
  120.6 2.4 %pad_slice_fusion = bf16[512,1024]{1,0:T(8,128)(2,1)} fusion(bf16[512,1024]{1,0:T(8,128)(2,1)} %shard_map.100), kind=kLoop, calls=%fused_computation.1 | loop fusion | bytes 2097152 | tf_op jit(solution)/shard_map/pad | solution.py:719
  (8 shorter events, 0.1 us)
Async XLA Ops:
  0.0 1.0 copy-start

commit v9 on v7

--- a/solution.py
+++ b/solution.py
@@ -36,8 +36,8 @@
     group,
     cap,
     scale,
-    ask_ref,
-    plan_ref,
+    ids_ref,
+    entry_ref,
     data_ref,
     live_ref,
     gain_ref,
@@ -47,6 +47,8 @@
     out_hbm,
     kv_hbm,
     mix_ref,
+    ask_ref,
+    plan_ref,
     base,
     asked,
     asked_s,
@@ -136,6 +138,41 @@
     for layer in range(layers):
         wall[layer, :, :, mine] = own[layer]
     base[...] = jnp.transpose(data_ref[...], (1, 0, 2))
+    per_shard = base.shape[0]
+    slots = ids_ref.shape[1]
+    requests = ids_ref.shape[0] * slots
+    size = requests // batches
+    holders, targets, places = [], [], []
+    earlier = jnp.int32(0)
+    shard_of = lax.broadcasted_iota(jnp.int32, ask_ref.shape, 0)
+    lane_of = lax.broadcasted_iota(jnp.int32, ask_ref.shape, 2)
+    table = jnp.zeros(ask_ref.shape, jnp.int32)
+    for n in range(requests):
+        located = entry_ref[ids_ref[n // slots, n % slots]]
+        holder, within = lax.div(located, per_shard), lax.rem(located, per_shard)
+        standing = jnp.int32(0)
+        for other in holders:
+            standing += jnp.where(other == holder, 1, 0)
+        is_early = jnp.where(standing < first, jnp.where(earlier < size, 1, 0), 0)
+        places.append(
+            jnp.minimum(
+                jnp.where(is_early == 1, earlier, size + n - jnp.minimum(earlier, size)),
+                requests - 1,
+            )
+        )
+        earlier += jnp.where(standing < first, 1, 0)
+        holders.append(holder)
+        targets.append(holder * cap + jnp.minimum(standing, cap - 1))
+        table = jnp.where((shard_of == holder) & (lane_of == standing), within, table)
+    ask_ref[...] = table
+    for spot in range(requests):
+        target, block = jnp.int32(0), jnp.int32(0)
+        for n in range(requests):
+            target = jnp.where(places[n] == spot, targets[n], target)
+            block = jnp.where(places[n] == spot, n // slots, block)
+        plan_ref[spot] = target
+        plan_ref[requests + spot] = block
+        plan_ref[2 * requests + spot] = places[spot]
     pl.semaphore_wait(barrier, shards + group - 2)
 
     def ask(k):
@@ -283,7 +320,7 @@
     def chosen(batch, number):
         place = plan_ref[batch * group + number]
         holder, slot = place // cap, lax.rem(place, cap)
-        return both[holder, slot] if batch else early[holder, slot]
+        return both[holder, slot] if batch else early[holder, jnp.minimum(slot, first - 1)]
 
     def keep_early(k, carry):
         both[k, pl.ds(0, first)] = early[k]
@@ -500,20 +537,21 @@
 
     lax.fori_loop(0, batches * chips, step, 0)
 
-    def combine(block, carry):
-        at = 2 * batches * group + 2 * block
-        one, two = plan_ref[at], plan_ref[at + 1]
-        alive = (live_ref[block] > 1).astype(jnp.float32)
-        span = pl.ds(pl.multiple_of(block * BL, BL), BL)
-        for h in range(heads_local):
-            lanes = pl.ds(h * pair, pair)
-            mixed = sums[one, :, lanes] + sums[two, :, lanes] * alive
-            mix_ref[span, pl.ds(h * head, head)] = (mixed[:, :head] / mixed[:, head:]).astype(
-                jnp.bfloat16
-            )
-        return carry
-
-    lax.fori_loop(0, blocks, combine, 0)
+    def combine(h, carry):
+        wide = pl.ds(pl.multiple_of(h * pair, pair), pair)
+        stage[pl.ds(0, BL)] = jnp.zeros((BL, head), jnp.float32)
+        for block in range(blocks):
+            one = plan_ref[2 * requests + slots * block]
+            two = plan_ref[2 * requests + slots * block + 1]
+            alive = (live_ref[block] > 1).astype(jnp.float32)
+            mixed = sums[one, :, wide] + sums[two, :, wide] * alive
+            stage[pl.ds(BL - 1 + block * BL, BL)] = mixed[:, :head] / mixed[:, head:]
+        mix_ref[:, pl.ds(pl.multiple_of(h * head, head), head)] = stage[pl.ds(0, tokens)].astype(
+            jnp.bfloat16
+        )
+        return carry
+
+    lax.fori_loop(0, heads_local, combine, 0)
     for batch in range(batches):
         for number in range(14):
             place = chunk_place(batch, me, 0)
@@ -524,7 +562,7 @@
         copy.wait_send()
 
 
-def retrieve(shards, group, cap, ask, plan, data, live, gain, final, query, own, out, kv):
+def retrieve(shards, group, cap, ids, entry_rows, data, live, gain, final, query, own, out, kv):
     positions, per_shard, head = data.shape
     layers, features = gain.shape
     batches = 2
@@ -536,9 +574,11 @@
     return pl.pallas_call(
         functools.partial(kernel, shards, group, cap, 3.0 / math.sqrt(head) * math.log2(math.e)),
         out_shape=jax.ShapeDtypeStruct(query.shape, bf16),
-        in_specs=[VMEM, SMEM, VMEM, SMEM, VMEM, VMEM, VMEM, ANY, ANY, ANY],
+        in_specs=[SMEM, SMEM, VMEM, SMEM, VMEM, VMEM, VMEM, ANY, ANY, ANY],
         out_specs=VMEM,
         scratch_shapes=[
+            pltpu.VMEM((shards, 1, 128), jnp.int32),
+            pltpu.SMEM((3 * ids.shape[0] * ids.shape[1],), jnp.int32),
             pltpu.VMEM((per_shard, positions, head), bf16),
             pltpu.VMEM((shards, 1, 128), jnp.int32),
             pltpu.SMEM((shards, 1, 128), jnp.int32),
@@ -582,7 +622,7 @@
         compiler_params=pltpu.CompilerParams(
             collective_id=0, has_side_effects=True, vmem_limit_bytes=60 * 2**20
         ),
-    )(ask, plan, data, live, gain, final, query, own, out, kv)
+    )(ids, entry_rows, data, live, gain, final, query, own, out, kv)
 
 
 def on_device(
@@ -599,40 +639,14 @@
 ):
     shards = lax.axis_size("db")
     group = lax.axis_size(GROUP)
-    per_shard = database.shape[1]
-    wanted = neighbour_ids.reshape(-1)
-    requests = wanted.shape[0]
+    requests = neighbour_ids.shape[0] * neighbour_ids.shape[1]
     capacity = max(2, (requests + shards - 1) // shards)
-    located = jnp.take(entry_rows, wanted)
-    holder = located // per_shard
-    within = located % per_shard
-    ordinal = jnp.arange(requests)
-    before = (holder[:, None] == holder[None, :]) & (ordinal[None, :] < ordinal[:, None])
-    standing = jnp.sum(before.astype(jnp.int32), axis=1)
-    target = holder * capacity + standing
-    early = standing < capacity // 2
-    earlier = jnp.sum((early[None, :] & (ordinal[None, :] < ordinal[:, None])).astype(jnp.int32), axis=1)
-    batch_size = requests // 2
-    place = jnp.where(
-        early & (earlier < batch_size),
-        earlier,
-        batch_size + ordinal - jnp.minimum(earlier, batch_size),
-    )
-    seated = (place[None, :] == ordinal[:, None]).astype(jnp.int32)
-    block_of = ordinal // neighbour_ids.shape[1]
-    plan = jnp.concatenate(
-        [jnp.sum(seated * target[None, :], axis=1), jnp.sum(seated * block_of[None, :], axis=1), place]
-    )
-    buckets = jnp.arange(shards)[:, None] * capacity + jnp.arange(128)[None, :]
-    inside = jnp.arange(128)[None, :, None] < capacity
-    matched = ((target[None, None, :] == buckets[:, :, None]) & inside).astype(jnp.int32)
-    outgoing = jnp.sum(matched * within[None, None, :], axis=2).reshape(shards, 1, 128)
-    mixed = retrieve(
+    return retrieve(
         shards,
         group,
         capacity,
-        outgoing,
-        plan,
+        neighbour_ids,
+        entry_rows,
         database,
         live_counts,
         enc_gain,
@@ -642,7 +656,6 @@
         enc_out,
         kv_weight,
     )
-    return lax.pad(mixed, jnp.zeros((), mixed.dtype), ((BL - 1, 1 - BL, 0), (0, 0, 0)))
 
 
 def solution(mesh):

time: 114 us -> 112 us (0.982)
  other arithmetic: 1.98 us -> 0 us
    unnamed x3 -> x2, local copies, waits for them, and re-layouts: 0.76 us -> 3.61 us
    pad x1 -> x0, local copies, waits for them, and re-layouts: 2.39 us -> none  [on_device(): lax.pad(mixed, jnp.zeros((), mixed.dtype), ((BL - 1, 1 - BL, 0), (0, 0, 0)))]
    reduce_sum x4 -> x0, other arithmetic: 1.18 us -> none  [the longest x1 0.76 us: on_device(): jnp.sum(matched * within[None, None, :], axis=2).reshape(shards, 1, 128)]
where the time goes in v9:
time: 112 us
  Pallas kernels  108 us (96%)
  local copies, waits for them, and re-layouts  3.61 us (3%)
    pallas_call x1, Pallas kernels, retrieve(): pl.pallas_call(functools.partial(kernel, shards, group, cap, 3.0 / math.s...  108 us
    unnamed x2, local copies, waits for them, and re-layouts  3.61 us

profile of v9, /device:TPU:1, one launch (start us, length us, event | category | flops | bytes accessed | tf_op | source)
XLA Modules:
  0.0 111.7 jit_solution(2335836184759761470)
XLA Ops:
  0.0 1.3 %copy.11.ids_ref = s32[8,2]{1,0:T(8,128)} copy(s32[8,2]{0,1:T(2,128)} %param.12) | data formatting | bytes 128 | tf_op args[2]
  1.3 108.1 %shard_map.100 = bf16[512,1024]{1,0:T(8,128)(2,1)} custom-call(s32[8,2]{1,0:T(8,128)} %copy.11.ids_ref, s32[1024]{0:T(1024)} %entry_ref.1, bf16[128,32,128]{2,1,0:T(8,128)(2,1)} %data_ref.1, s32[8]{0:T(128)} %live_ref.1, f32[2,1024]{1,0:T(2,128)} %gain_ref.1, f32[1,1024]{1,0:T(1,128)} %bitcast.3, bf16[512,1024]{1,0:T(8,128)(2,1)} %query_ref.1, ...), custom_call_target="tpu_custom_call" | custom-call | tf_op jit(solution)/shard_map/pallas_call | solution.py:574
  109.5 2.3 %copy.13 = bf16[512,1024]{1,0:T(8,128)(2,1)} copy(bf16[512,1024]{1,0:T(8,128)(2,1)} %shard_map.100) | data formatting | bytes 2097152

commit v10 on v9

--- a/solution.py
+++ b/solution.py
@@ -507,28 +507,28 @@
         @pl.when(number == 3)
         def _():
             twin_wait(0, up_twin)
+
+        @pl.when(number == 4)
+        def _():
+            relay_near(1)
             relay_far(0)
-
-        @pl.when(number == 4)
-        def _():
-            relay_near(1)
+            twin_wait(1, down_twin)
+
+        @pl.when(number == 5)
+        def _():
+            twin_wait(1, up_twin)
+
+        @pl.when(number == 6)
+        def _():
+            relay_far(1)
             twin_wait(0, far_twin)
 
-        @pl.when(number == 5)
-        def _():
-            twin_wait(1, down_twin)
-
-        @pl.when(number == 6)
-        def _():
-            relay_far(1)
-            twin_wait(1, up_twin)
-
         @pl.when(number == 7)
         def _():
             twin_wait(1, far_twin)
 
-        batch = jnp.where(number == 1, 1, jnp.where(number >= 5, 1, 0))
-        turn = jnp.where(number < 2, 0, jnp.where(number < 5, number - 1, number - 4))
+        batch = jnp.where(number < 2, number, jnp.where(number < 6, number // 2 - 1, number - 6))
+        turn = jnp.where(number < 2, 0, jnp.where(number < 6, 1 + lax.rem(number, 2), 3))
         chip = jnp.where(
             turn == 0, y, jnp.where(turn == 1, down, jnp.where(turn == 2, up, far))
         )

time: 112 us -> 110 us (0.982)
  Pallas kernels: 108 us -> 106 us
    pallas_call x1, Pallas kernels: 108 us -> 106 us  [retrieve(): pl.pallas_call(functools.partial(kernel, shards, group, cap, 3.0 / math.s...]
where the time goes in v10:
time: 110 us; the launch traced here: 109 us
  Pallas kernels  106 us (96%)
  local copies, waits for them, and re-layouts  3.61 us (3%)
    pallas_call x1, Pallas kernels, retrieve(): pl.pallas_call(functools.partial(kernel, shards, group, cap, 3.0 / math.s...  106 us
    unnamed x2, local copies, waits for them, and re-layouts  3.61 us

profile of v10, /device:TPU:1, one launch (start us, length us, event | category | flops | bytes accessed | tf_op | source)
XLA Modules:
  0.0 109.5 jit_solution(14366305385533199136)
XLA Ops:
  0.0 1.3 %copy.11.ids_ref = s32[8,2]{1,0:T(8,128)} copy(s32[8,2]{0,1:T(2,128)} %param.12) | data formatting | bytes 128 | tf_op args[2]
  1.3 105.8 %shard_map.100 = bf16[512,1024]{1,0:T(8,128)(2,1)} custom-call(s32[8,2]{1,0:T(8,128)} %copy.11.ids_ref, s32[1024]{0:T(1024)} %entry_ref.1, bf16[128,32,128]{2,1,0:T(8,128)(2,1)} %data_ref.1, s32[8]{0:T(128)} %live_ref.1, f32[2,1024]{1,0:T(2,128)} %gain_ref.1, f32[1,1024]{1,0:T(1,128)} %bitcast.3, bf16[512,1024]{1,0:T(8,128)(2,1)} %query_ref.1, ...), custom_call_target="tpu_custom_call" | custom-call | tf_op jit(solution)/shard_map/pallas_call | solution.py:574
  107.2 2.3 %copy.13 = bf16[512,1024]{1,0:T(8,128)(2,1)} copy(bf16[512,1024]{1,0:T(8,128)(2,1)} %shard_map.100) | data formatting | bytes 2097152
